TPU v7x, 32 devices: a whole 2x2x4 slice. The times are simulated.
32 devices in a mesh: res: 8 (over z, x), rep: 4 (over y, core).
Axes of the slice: x: 2, y: 2, z: 4, core: 2. Of those that a mesh axis runs over, the one named last changes fastest.
Arguments:
- pair: bfloat16 [4, 384, 384, 128], P('rep', 'res'), may hold values from -64 to 64
- residue_mask: int32 [4, 384], P('rep'), may hold values from 0 to 1, as said below
- bin_targets: int32 [4, 384, 384], P('rep', 'res'), may hold values from 0 to 63
- gain_in: float32 [128], replicated, may hold values from 0.1 to 1.9
- left_proj: bfloat16 [128, 128], replicated, may hold values from -0.5 to 0.5
- left_gate: bfloat16 [128, 128], replicated, may hold values from -0.5 to 0.5
- right_proj: bfloat16 [128, 128], replicated, may hold values from -0.5 to 0.5
- right_gate: bfloat16 [128, 128], replicated, may hold values from -0.5 to 0.5
- gate_weight: bfloat16 [128, 128], replicated, may hold values from -0.5 to 0.5
- gain_out: float32 [128], replicated, may hold values from 0.1 to 1.9
- out_weight: bfloat16 [128, 128], replicated, may hold values from -0.5 to 0.5
- head_weight: bfloat16 [128, 64], replicated, may hold values from -2 to 2
- head_bias: float32 [64], replicated, may hold values from -4 to 4
Outputs:
- updated_pair: bfloat16 [4, 384, 384, 128], P('rep', 'res')
- pair_grad: bfloat16 [4, 384, 384, 128], P('rep', 'res')
- head_grad: float32 [128, 64], replicated
- bias_grad: float32 [64], replicated
- mean_loss: float32 [1], replicated
Inputs may be any that keep to these rules, and one draw needn't show every extreme that they name: `residue_mask`: 1 marks a resolved residue; the last residue of each crop is 1.
All inputs are finite; a program needn't handle non-finite values.
Results may differ from a plain program's by a relative error of at most 0.0065.
The roundings to bfloat16 on the way count: a program that leaves them out, or rounds other values in their place, can miss the bound.
Values may be sent and summed in bfloat16 or wider, within the bound.
A program may use at most 128 MiB of HBM per device.

v0:
```python
import jax
import jax.numpy as jnp
from jax import lax
from jax.sharding import PartitionSpec as P


def layer_norm(values, reduce_axis):
    average = jnp.mean(values, axis=reduce_axis, keepdims=True)
    centered = values - average
    variance = jnp.mean(centered * centered, axis=reduce_axis, keepdims=True)
    return centered * lax.rsqrt(variance + 1e-05)


def body(
    pair,
    residue_mask,
    bin_targets,
    gain_in,
    left_proj,
    left_gate,
    right_proj,
    right_gate,
    gate_weight,
    gain_out,
    out_weight,
    head_weight,
    head_bias,
):
    row_count = pair.shape[1]
    crop_pair = pair[0]
    targets = bin_targets[0]
    row_start = lax.axis_index("res") * row_count
    resolved = residue_mask[0].astype(jnp.float32)
    row_mask = lax.dynamic_slice_in_dim(resolved, row_start, row_count)
    pair_mask = row_mask[:, None] * resolved[None, :]
    pair_float = crop_pair.astype(jnp.float32)
    normed = (layer_norm(pair_float, 2) * gain_in).astype(jnp.bfloat16)

    def factor(project_weight, gating_weight):
        projected = jnp.einsum(
            "rkd,dc->crk", normed, project_weight, preferred_element_type=jnp.float32
        )
        gated = jax.nn.sigmoid(
            jnp.einsum("rkd,dc->crk", normed, gating_weight, preferred_element_type=jnp.float32)
        )
        return (gated * projected * pair_mask[None]).astype(jnp.bfloat16)

    left_factor = factor(left_proj, left_gate)
    right_factor = factor(right_proj, right_gate)
    left_units, right_units = (
        lax.all_to_all(left_factor, "res", split_axis=0, concat_axis=1, tiled=True),
        lax.all_to_all(right_factor, "res", split_axis=0, concat_axis=1, tiled=True),
    )
    by_units = jnp.einsum(
        "cik,cjk->cij", left_units, right_units, preferred_element_type=jnp.float32
    ).astype(jnp.bfloat16)
    triangle_out = lax.all_to_all(by_units, "res", split_axis=1, concat_axis=0, tiled=True)
    normed_tri = (layer_norm(triangle_out.astype(jnp.float32), 0) * gain_out[:, None, None]).astype(
        jnp.bfloat16
    )
    update = jnp.einsum("crk,cd->rkd", normed_tri, out_weight, preferred_element_type=jnp.float32)
    gating = jax.nn.sigmoid(
        jnp.einsum("rkd,de->rke", normed, gate_weight, preferred_element_type=jnp.float32)
    )
    updated = (pair_float + gating * update).astype(jnp.bfloat16)
    mirrored = jnp.swapaxes(
        lax.all_to_all(updated, "res", split_axis=1, concat_axis=0, tiled=True), 0, 1
    )
    symmetric = (updated.astype(jnp.float32) + mirrored.astype(jnp.float32)).astype(jnp.bfloat16)
    logits = (
        jnp.einsum("rkd,dn->nrk", symmetric, head_weight, preferred_element_type=jnp.float32)
        + head_bias[:, None, None]
    )
    top_logit = jnp.max(logits, axis=0, keepdims=True)
    log_total = jnp.log(jnp.sum(jnp.exp(logits - top_logit), axis=0, keepdims=True)) + top_logit
    probability = jnp.exp(logits - log_total)
    bin_index = lax.broadcasted_iota(jnp.int32, (logits.shape[0], 1, 1), 0)
    target_hot = (targets[None] == bin_index).astype(jnp.float32)
    dlogits = (pair_mask[None] * (probability - target_hot)).astype(jnp.bfloat16)
    pair_term = jnp.einsum("nrk,dn->rkd", dlogits, head_weight, preferred_element_type=jnp.float32)
    mirror_term = jnp.swapaxes(
        lax.all_to_all(
            pair_term.astype(jnp.bfloat16), "res", split_axis=1, concat_axis=0, tiled=True
        ).astype(pair_term.dtype),
        0,
        1,
    )
    pair_grad = (pair_term + mirror_term).astype(jnp.bfloat16)
    head_part = jnp.einsum("rkd,nrk->dn", symmetric, dlogits, preferred_element_type=jnp.float32)
    bias_part = jnp.sum(dlogits.astype(jnp.float32), axis=(1, 2))
    loss_part = jnp.sum(pair_mask * (log_total[0] - jnp.sum(target_hot * logits, axis=0)))
    count_part = jnp.sum(pair_mask)
    head_total, bias_total, loss_total, count = lax.psum(
        (head_part, bias_part, loss_part, count_part), ("res", "rep")
    )
    mean_loss = jnp.reshape(loss_total / count, (1,))
    return (updated[None], pair_grad[None], head_total / count, bias_total / count, mean_loss)


def solution(mesh):
    return jax.shard_map(
        body,
        mesh=mesh,
        in_specs=(
            P("rep", "res", None, None),
            P("rep", None),
            P("rep", "res", None),
            P(),
            P(),
            P(),
            P(),
            P(),
            P(),
            P(),
            P(),
            P(),
            P(),
        ),
        out_specs=(P("rep", "res", None, None), P("rep", "res", None, None), P(), P(), P()),
        check_vma=False,
    )
```

profile of v0, /device:TPU:0, one launch (start us, length us, event | category | flops | bytes accessed | tf_op | source)
XLA Modules:
  0.0 692.3 jit_solution(8194600087287086704)
XLA Ops:
  0.7 0.7 convert_element_type.98
  1.3 0.7 convert_reduce_fusion.2
  2.1 3.8 convert_reduce_fusion
  5.9 5.5 fusion.4
  11.4 0.1 dynamic-slice_bitcast_fusion
  11.5 0.1 add_rsqrt_fusion.1
  11.6 9.5 %fusion.30 = f32[48,384,128]{2,1,0:T(8,128)S(1)} fusion(bf16[128,128]{1,0:T(8,128)(2,1)S(1)} %copy-done, bf16[1,48,384,128]{3,2,1,0:T(8,128)(2,1)} %param.13, f32[128]{0:T(128)S(1)} %copy-done.12, f32[48,384]{1,0:T(8,128)S(1)} %get-tuple-element.20, f32[48,384]{1,0:T(8,128)S(1)} %broadcast_multiply_fusion.2), kind=kOutput, calls=%fused_computation.55 | convolution fusion | flops 615776256 | bytes 14336512 | tf_op jit(solution)/shard_map/rkd,dc->crk/dot_general | solution.py:44
  21.1 10.5 %fusion.23 = bf16[128,48,384]{0,2,1:T(8,128)(2,1)} fusion(f32[48,384]{1,0:T(8,128)S(1)} %get-tuple-element.21, f32[48,384,128]{2,1,0:T(8,128)S(1)} %fusion.30, bf16[128,128]{1,0:T(8,128)(2,1)S(1)} %copy-done.17, bf16[1,48,384,128]{3,2,1,0:T(8,128)(2,1)S(1)} %bitcast.133, f32[128]{0:T(128)S(1)} %copy-done.12, f32[48,384]{1,0:T(8,128)S(1)} %get-tuple-element.20, ...), kind=kOutput, calls=%fused_computation.38 | convolution fusion | flops 629932032 | bytes 19128832 | tf_op jit(solution)/shard_map/rkd,dc->crk/dot_general | solution.py:40
  31.7 7.0 %copy.41 = bf16[128,48,384]{2,1,0:T(8,128)(2,1)} copy(bf16[128,48,384]{0,2,1:T(8,128)(2,1)} %fusion.23) | data formatting | bytes 9437184 | tf_op jit(solution)/shard_map/convert_element_type | solution.py:46
  38.6 7.4 %all-to-all-start = ((bf16[128,48,384]{2,1,0:T(8,128)(2,1)}), bf16[128,48,384]{2,1,0:T(8,128)(2,1)}, u32[]{:S(2)}, u32[]{:S(2)}) async-start(bf16[128,48,384]{2,1,0:T(8,128)(2,1)} %copy.41), calls=%async_computation | async-start | bytes 9437184 | tf_op jit(solution)/shard_map/all_to_all | solution.py:51
  46.1 9.5 %fusion.27 = f32[48,384,128]{2,1,0:T(8,128)S(1)} fusion(bf16[128,128]{1,0:T(8,128)(2,1)S(1)} %copy-done.8, bf16[1,48,384,128]{3,2,1,0:T(8,128)(2,1)} %param.13, f32[128]{0:T(128)S(1)} %copy-done.12, f32[48,384]{1,0:T(8,128)S(1)} %get-tuple-element.20, f32[48,384]{1,0:T(8,128)S(1)} %broadcast_multiply_fusion.2), kind=kOutput, calls=%fused_computation.52 | convolution fusion | flops 615776256 | bytes 14336512 | tf_op jit(solution)/shard_map/rkd,dc->crk/dot_general | solution.py:44
  55.6 10.5 %fusion.24 = bf16[128,48,384]{0,2,1:T(8,128)(2,1)} fusion(f32[48,384]{1,0:T(8,128)S(1)} %get-tuple-element.21, f32[48,384,128]{2,1,0:T(8,128)S(1)} %fusion.27, bf16[128,128]{1,0:T(8,128)(2,1)S(1)} %copy-done.18, bf16[1,48,384,128]{3,2,1,0:T(8,128)(2,1)S(1)} %bitcast.135, f32[128]{0:T(128)S(1)} %copy-done.12, f32[48,384]{1,0:T(8,128)S(1)} %get-tuple-element.20, ...), kind=kOutput, calls=%fused_computation.39 | convolution fusion | flops 629932032 | bytes 19128832 | tf_op jit(solution)/shard_map/rkd,dc->crk/dot_general | solution.py:40
  66.1 7.2 %copy.43 = bf16[128,48,384]{2,1,0:T(8,128)(2,1)} copy(bf16[128,48,384]{0,2,1:T(8,128)(2,1)} %fusion.24) | data formatting | bytes 9437184 | tf_op jit(solution)/shard_map/convert_element_type | solution.py:46
  73.4 77.2 %all-to-all-done = bf16[128,48,384]{2,1,0:T(8,128)(2,1)} async-done(((bf16[128,48,384]{2,1,0:T(8,128)(2,1)}), bf16[128,48,384]{2,1,0:T(8,128)(2,1)}, u32[]{:S(2)}, u32[]{:S(2)}) %all-to-all-start) | async-done | bytes 4718624 | tf_op jit(solution)/shard_map/all_to_all | solution.py:51
  150.5 4.6 all-to-all-start.1
  155.2 5.2 copy.42
  160.4 98.5 %all-to-all-done.1 = bf16[128,48,384]{2,1,0:T(8,128)(2,1)} async-done(((bf16[128,48,384]{2,1,0:T(8,128)(2,1)}), bf16[128,48,384]{2,1,0:T(8,128)(2,1)}, u32[]{:S(2)}, u32[]{:S(2)}) %all-to-all-start.1) | async-done | bytes 4718624 | tf_op jit(solution)/shard_map/all_to_all | solution.py:52
  258.9 3.2 copy.44
  262.1 0.5 copy-done.4
  262.7 3.4 convolution_convert_fusion
  266.1 2.8 copy.45
  268.9 108.1 %all_to_all.63 = bf16[16,384,384]{2,0,1:T(8,128)(2,1)S(1)} all-to-all(bf16[16,384,384]{2,0,1:T(8,128)(2,1)S(1)} %copy.45), channel_id=1, replica_groups=mesh['res'=8,'rep'=4] {'res'}, dimensions={1} | all-to-all | bytes 9437184 | tf_op jit(solution)/shard_map/all_to_all | solution.py:57
  377.0 1.1 copy.46
  378.2 0.7 fusion.13
  378.9 1.0 convert_bitcast_fusion.1
  379.9 1.3 multiply_reduce_fusion
  381.3 4.5 copy.47
  385.8 5.0 fusion.12
  390.9 1.5 fusion.21
  392.4 9.3 %fusion.7 = bf16[48,384,128]{2,1,0:T(8,128)(2,1)S(1)} fusion(bf16[1,48,384,128]{3,2,1,0:T(8,128)(2,1)S(1)} %bitcast.137, f32[48,384,128]{2,1,0:T(8,128)S(1)} %fusion.21, bf16[128,128]{1,0:T(8,128)(2,1)S(1)} %copy-done.19, f32[128]{0:T(128)S(1)} %copy-done.12, f32[48,384]{1,0:T(8,128)S(1)} %get-tuple-element.20, f32[48,384]{1,0:T(8,128)S(1)} %broadcast_multiply_fusion.2), kind=kOutput, calls=%fused_computation.9 | convolution fusion | flops 632291328 | bytes 19055104 | tf_op jit(solution)/shard_map/rkd,de->rke/dot_general | solution.py:63
  401.7 3.0 copy.49
  404.7 107.9 %all_to_all.64 = bf16[48,384,128]{2,0,1:T(8,128)(2,1)S(1)} all-to-all(bf16[48,384,128]{2,0,1:T(8,128)(2,1)S(1)} %copy.49), channel_id=1, replica_groups=mesh['res'=8,'rep'=4] {'res'}, dimensions={1} | all-to-all | bytes 9437184 | tf_op jit(solution)/shard_map/all_to_all | solution.py:67
  512.6 4.9 copy.50
  517.5 5.4 fusion.9
  523.0 1.8 bitcast_reduce_fusion
  524.8 0.4 copy-done.3
  525.2 2.3 fusion.20
  527.5 0.7 multiply_reduce_fusion.1
  528.2 2.7 convert_reduce_fusion.1
  530.9 4.5 fusion.43
  535.4 5.2 copy.51
  540.6 4.9 all-to-all-start.4
  545.4 3.4 convolution_bitcast_fusion
  548.8 120.6 %all-reduce = (f32[128,64]{0,1:T(8,128)S(1)}, f32[]{:T(128)}, f32[64]{0:T(128)S(1)}, f32[]{:T(128)}) all-reduce(f32[128,64]{0,1:T(8,128)S(1)} %convolution_bitcast_fusion, f32[]{:T(128)} %get-tuple-element.8, f32[64]{0:T(128)S(1)} %get-tuple-element.13, f32[]{:T(128)} %get-tuple-element.7), channel_id=1, replica_groups=mesh['res'=8,'rep'=4] {'res','rep'}, use_global_device_ids=true, to_apply=%region_6.0 | all-reduce | flops 8258 | bytes 66064 | tf_op jit(solution)/shard_map/psum | solution.py:93
  670.7 1.1 broadcast_divide_fusion.1
  671.8 1.2 broadcast_divide_fusion
  673.1 7.2 %copy.52 = f32[48,8,48,128]{3,0,1,2:T(8,128)} copy(bf16[48,8,48,128]{3,0,2,1:T(8,128)(2,1)} %bitcast.40) | data formatting | bytes 14155776 | tf_op jit(solution)/shard_map/transpose | solution.py:81
  680.3 10.4 %fusion.8 = bf16[48,384,128]{2,1,0:T(8,128)(2,1)} fusion(f32[48,384,128]{2,1,0:T(8,128)} %get-tuple-element.19, f32[48,8,48,128]{3,0,1,2:T(8,128)} %copy.52), kind=kLoop, calls=%fused_computation.11 | loop fusion | flops 4718592 | bytes 23592960 | tf_op jit(solution)/shard_map/convert_element_type | solution.py:88
  (57 shorter events, 0.2 us)
Async XLA Ops:
  0.6 10.9 %copy-start = (bf16[128,128]{1,0:T(8,128)(2,1)S(1)}, bf16[128,128]{1,0:T(8,128)(2,1)}, u32[]{:S(2)}) copy-start(bf16[128,128]{1,0:T(8,128)(2,1)} %param.18) | copy-start | bytes 98308
  2.0 9.4 %copy-start.10 = (f32[384]{0:T(512)}, f32[384]{0:T(512)S(1)}, u32[]{:S(2)}) copy-start(f32[384]{0:T(512)S(1)} %convert_reduce_fusion.2) | copy-start | bytes 4612
  2.0 3.8 copy-start.2
  2.1 9.5 %copy-start.12 = (f32[128]{0:T(128)S(1)}, f32[128]{0:T(128)}, u32[]{:S(2)}) copy-start(f32[128]{0:T(128)} %param.16) | copy-start | bytes 1540
  5.9 15.2 %slice-start = ((s8[4718592]{0:T(1024)(128)(4,1)}), s8[524288]{0:T(1024)(128)(4,1)S(1)}, s32[]{:S(2)}) async-start(s8[4718592]{0:T(1024)(128)(4,1)} %bitcast.132), calls=%async_computation.5 | async-start | bytes 1048576
  11.5 9.6 %copy-start.14 = (f32[48]{0:T(128)}, f32[48]{0:T(128)S(1)}, u32[]{:S(2)}) copy-start(f32[48]{0:T(128)S(1)} %dynamic-slice_bitcast_fusion) | copy-start | bytes 580
  11.6 9.5 %slice-start.1 = ((s8[4718592]{0:T(1024)(128)(4,1)}), s8[4194304]{0:T(1024)(128)(4,1)S(1)}, s32[]{:S(2)}) async-start(s8[4718592]{0:T(1024)(128)(4,1)} %bitcast.132), calls=%async_computation.6 | async-start | bytes 8388608
  11.6 9.5 %copy-start.17 = (bf16[128,128]{1,0:T(8,128)(2,1)S(1)}, bf16[128,128]{1,0:T(8,128)(2,1)}, u32[]{:S(2)}) copy-start(bf16[128,128]{1,0:T(8,128)(2,1)} %param.17) | copy-start | bytes 98308
  38.6 7.4 %copy-start.8 = (bf16[128,128]{1,0:T(8,128)(2,1)S(1)}, bf16[128,128]{1,0:T(8,128)(2,1)}, u32[]{:S(2)}) copy-start(bf16[128,128]{1,0:T(8,128)(2,1)} %param.20) | copy-start | bytes 98308
  38.6 16.9 %slice-start.2 = ((s8[4718592]{0:T(1024)(128)(4,1)}), s8[524288]{0:T(1024)(128)(4,1)S(1)}, s32[]{:S(2)}) async-start(s8[4718592]{0:T(1024)(128)(4,1)} %bitcast.134), calls=%async_computation.7 | async-start | bytes 1048576
  38.6 111.9 %all-to-all-start = ((bf16[128,48,384]{2,1,0:T(8,128)(2,1)}), bf16[128,48,384]{2,1,0:T(8,128)(2,1)}, u32[]{:S(2)}, u32[]{:S(2)}) async-start(bf16[128,48,384]{2,1,0:T(8,128)(2,1)} %copy.41), calls=%async_computation | async-start | bytes 9437184 | tf_op jit(solution)/shard_map/all_to_all | solution.py:51
  46.0 9.5 %slice-start.3 = ((s8[4718592]{0:T(1024)(128)(4,1)}), s8[4194304]{0:T(1024)(128)(4,1)S(1)}, s32[]{:S(2)}) async-start(s8[4718592]{0:T(1024)(128)(4,1)} %bitcast.134), calls=%async_computation.8 | async-start | bytes 8388608
  46.0 9.5 %copy-start.18 = (bf16[128,128]{1,0:T(8,128)(2,1)S(1)}, bf16[128,128]{1,0:T(8,128)(2,1)}, u32[]{:S(2)}) copy-start(bf16[128,128]{1,0:T(8,128)(2,1)} %param.19) | copy-start | bytes 98308
  150.5 108.4 %all-to-all-start.1 = ((bf16[128,48,384]{2,1,0:T(8,128)(2,1)}), bf16[128,48,384]{2,1,0:T(8,128)(2,1)}, u32[]{:S(2)}, u32[]{:S(2)}) async-start(bf16[128,48,384]{2,1,0:T(8,128)(2,1)} %copy.43), calls=%async_computation.1 | async-start | bytes 9437184 | tf_op jit(solution)/shard_map/all_to_all | solution.py:52
  258.9 3.8 copy-start.4
  381.2 4.6 copy-start.16
  381.3 11.1 %slice-start.4 = ((s8[4718592]{0:T(1024)(128)(4,1)}), s8[4194304]{0:T(1024)(128)(4,1)S(1)}, s32[]{:S(2)}) async-start(s8[4718592]{0:T(1024)(128)(4,1)} %bitcast.136), calls=%async_computation.9 | async-start | bytes 8388608
  385.8 5.0 copy-start.9
  385.8 6.5 slice-start.5
  390.8 1.5 copy-start.19
  401.7 115.8 %copy-start.5 = (bf16[48,384,128]{2,1,0:T(8,128)(2,1)}, bf16[48,384,128]{2,1,0:T(8,128)(2,1)S(1)}, u32[]{:S(2)}) copy-start(bf16[48,384,128]{2,1,0:T(8,128)(2,1)S(1)} %fusion.7) | copy-start | bytes 14155780
  517.5 5.4 copy-start.7
  517.5 5.4 copy-start.13
  523.0 2.2 copy-start.3
  523.0 2.2 copy-start.6
  525.2 2.3 copy-start.11
  525.2 2.3 copy-start.15
  540.6 132.5 %all-to-all-start.4 = ((bf16[48,384,128]{2,0,1:T(8,128)(2,1)}), bf16[48,384,128]{2,0,1:T(8,128)(2,1)}, u32[]{:S(2)}, u32[]{:S(2)}) async-start(bf16[48,384,128]{2,0,1:T(8,128)(2,1)} %copy.51), calls=%async_computation.4 | async-start | bytes 9437184 | tf_op jit(solution)/shard_map/all_to_all | solution.py:82
  680.3 10.4 %copy-start.1 = (bf16[128,128]{1,0:T(8,128)(2,1)S(1)}, bf16[128,128]{1,0:T(8,128)(2,1)}, u32[]{:S(2)}) copy-start(bf16[128,128]{1,0:T(8,128)(2,1)} %param.18) | copy-start | bytes 98308
where the time goes:
time: 701 us; the launch traced here: 692 us
  blocking collectives  337 us (48%)
  waiting for transfers between devices  176 us (25%)
  matrix products  63.9 us (9%)
  local copies, waits for them, and re-layouts  52.6 us (8%)
  other arithmetic  42.7 us (6%)
  starting transfers between devices  16.8 us (2%)
    psum x1, blocking collectives, body(): lax.psum((head_part, bias_part, loss_part, count_part), ('res', 'rep'))  121 us
    all_to_all x1, blocking collectives, body(): lax.all_to_all(by_units, 'res', split_axis=1, concat_axis=0, tiled=True)  108 us
    all_to_all x1, blocking collectives, body(): lax.all_to_all(updated, 'res', split_axis=1, concat_axis=0, tiled=True)  108 us
    all_to_all x1, waiting for transfers between devices, body(): lax.all_to_all(right_factor, 'res', split_axis=0, concat_axis=1, tiled=True)  98.5 us
    all_to_all x1, waiting for transfers between devices, body(): lax.all_to_all(left_factor, 'res', split_axis=0, concat_axis=1, tiled=True)  77.2 us
    dot_general x2, matrix products, factor(): jnp.einsum('rkd,dc->crk', normed, project_weight, preferred_element_type=...  21.1 us
    dot_general x2, matrix products, factor(): jnp.einsum('rkd,dc->crk', normed, gating_weight, preferred_element_type=j...  19 us
    convert_element_type x2, local copies, waits for them, and re-layouts, factor(): return (gated * projected * pair_mask[None]).astype(jnp.bfloat16)  14.2 us
  transfers between devices with their start and end apart: 3, of which 2 were waited for; matrix products, arithmetic and copies ran while one was open for 6% of the time, Pallas kernels for 0%

commit v1 on v0

--- a/solution.py
+++ b/solution.py
@@ -35,6 +35,9 @@
     pair_mask = row_mask[:, None] * resolved[None, :]
     pair_float = crop_pair.astype(jnp.float32)
     normed = (layer_norm(pair_float, 2) * gain_in).astype(jnp.bfloat16)
+    mirror_targets = jnp.swapaxes(
+        lax.all_to_all(targets, "res", split_axis=1, concat_axis=0, tiled=True), 0, 1
+    )
 
     def factor(project_weight, gating_weight):
         projected = jnp.einsum(
@@ -77,15 +80,14 @@
     bin_index = lax.broadcasted_iota(jnp.int32, (logits.shape[0], 1, 1), 0)
     target_hot = (targets[None] == bin_index).astype(jnp.float32)
     dlogits = (pair_mask[None] * (probability - target_hot)).astype(jnp.bfloat16)
-    pair_term = jnp.einsum("nrk,dn->rkd", dlogits, head_weight, preferred_element_type=jnp.float32)
-    mirror_term = jnp.swapaxes(
-        lax.all_to_all(
-            pair_term.astype(jnp.bfloat16), "res", split_axis=1, concat_axis=0, tiled=True
-        ).astype(pair_term.dtype),
-        0,
-        1,
-    )
-    pair_grad = (pair_term + mirror_term).astype(jnp.bfloat16)
+    mirror_hot = (mirror_targets[None] == bin_index).astype(jnp.float32)
+    mirror_dlogits = (pair_mask[None] * (probability - mirror_hot)).astype(jnp.bfloat16)
+    pair_grad = jnp.einsum(
+        "nrk,dn->rkd",
+        jnp.concatenate([dlogits, mirror_dlogits], axis=0),
+        jnp.concatenate([head_weight, head_weight], axis=1),
+        preferred_element_type=jnp.float32,
+    ).astype(jnp.bfloat16)
     head_part = jnp.einsum("rkd,nrk->dn", symmetric, dlogits, preferred_element_type=jnp.float32)
     bias_part = jnp.sum(dlogits.astype(jnp.float32), axis=(1, 2))
     loss_part = jnp.sum(pair_mask * (log_total[0] - jnp.sum(target_hot * logits, axis=0)))

time: 701 us -> 601 us (0.86)
  blocking collectives: 337 us -> 38.4 us
  waiting for transfers between devices: 176 us -> 381 us
  starting transfers between devices: 16.8 us -> 26.5 us
  other arithmetic: 42.7 us -> 34.3 us
    all_to_all x2 -> x0, blocking collectives: 216 us -> none  [the longest x1 108 us: body(): lax.all_to_all(by_units, 'res', split_axis=1, concat_axis=0, tiled=True)]
    all_to_all x1 -> x3, waiting for transfers between devices: 0.01 us -> 205 us  [the longest x1 103 us: body(): lax.all_to_all(by_units, 'res', split_axis=1, concat_axis=0, tiled=True)]
    psum x1, blocking collectives: 121 us -> 38.4 us  [body(): lax.psum((head_part, bias_part, loss_part, count_part), ('res', 'rep'))]
    all_to_all x1, waiting for transfers between devices: 77.2 us -> 98.5 us  [body(): lax.all_to_all(left_factor, 'res', split_axis=0, concat_axis=1, tiled=True)]
    all_to_all x1, waiting for transfers between devices: 98.5 us -> 77.5 us  [body(): lax.all_to_all(right_factor, 'res', split_axis=0, concat_axis=1, tiled=True)]
    convert_element_type x1 -> x0, other arithmetic: 10.4 us -> none  [body(): pair_grad = (pair_term + mirror_term).astype(jnp.bfloat16)]
    all_to_all x1 -> x3, starting transfers between devices: 4.85 us -> 14.5 us  [the longest x1 6.13 us: body(): lax.all_to_all(updated, 'res', split_axis=1, concat_axis=0, tiled=True)]
    transpose x1 -> x0, local copies, waits for them, and re-layouts: 7.22 us -> none  [body(): jnp.swapaxes(lax.all_to_all(pair_term.astype(jnp.bfloat16), 'res', split_...]
  transfers between devices with their start and end apart: 3 -> 5, of which waited for: 2 -> 4; matrix products, arithmetic and copies ran while one was open for 6% -> 11% of each run, Pallas kernels for 0% -> 0%
where the time goes in v1:
time: 601 us; the launch traced here: 599 us
  waiting for transfers between devices  381 us (63%)
  matrix products  62.4 us (10%)
  local copies, waits for them, and re-layouts  53 us (9%)
  blocking collectives  38.4 us (6%)
  other arithmetic  34.3 us (6%)
  starting transfers between devices  26.5 us (4%)
    all_to_all x1, waiting for transfers between devices, body(): lax.all_to_all(by_units, 'res', split_axis=1, concat_axis=0, tiled=True)  103 us
    all_to_all x1, waiting for transfers between devices, body(): lax.all_to_all(updated, 'res', split_axis=1, concat_axis=0, tiled=True)  102 us
    all_to_all x1, waiting for transfers between devices, body(): lax.all_to_all(left_factor, 'res', split_axis=0, concat_axis=1, tiled=True)  98.5 us
    all_to_all x1, waiting for transfers between devices, body(): lax.all_to_all(right_factor, 'res', split_axis=0, concat_axis=1, tiled=True)  77.5 us
    psum x1, blocking collectives, body(): lax.psum((head_part, bias_part, loss_part, count_part), ('res', 'rep'))  38.4 us
    dot_general x2, matrix products, factor(): jnp.einsum('rkd,dc->crk', normed, project_weight, preferred_element_type=...  21.1 us
    dot_general x2, matrix products, factor(): jnp.einsum('rkd,dc->crk', normed, gating_weight, preferred_element_type=j...  18.9 us
    convert_element_type x2, local copies, waits for them, and re-layouts, factor(): return (gated * projected * pair_mask[None]).astype(jnp.bfloat16)  14.1 us
  transfers between devices with their start and end apart: 5, of which 4 were waited for; matrix products, arithmetic and copies ran while one was open for 11% of the time, Pallas kernels for 0%

profile of v1, /device:TPU:0, one launch (start us, length us, event | category | flops | bytes accessed | tf_op | source)
XLA Modules:
  0.0 599.1 jit_solution(8317178820239090434)
XLA Ops:
  0.7 0.7 convert_element_type.91
  1.3 0.7 convert_reduce_fusion.2
  2.1 3.8 convert_reduce_fusion
  5.9 5.5 fusion.4
  11.6 9.5 %fusion.31 = f32[48,384,128]{2,1,0:T(8,128)S(1)} fusion(bf16[128,128]{1,0:T(8,128)(2,1)S(1)} %copy-done, bf16[1,48,384,128]{3,2,1,0:T(8,128)(2,1)} %param.13, f32[128]{0:T(128)S(1)} %copy-done.11, f32[48,384]{1,0:T(8,128)S(1)} %get-tuple-element.19, f32[48,384]{1,0:T(8,128)S(1)} %broadcast_multiply_fusion.2), kind=kOutput, calls=%fused_computation.58 | convolution fusion | flops 615776256 | bytes 14336512 | tf_op jit(solution)/shard_map/rkd,dc->crk/dot_general | solution.py:47
  21.1 10.6 %fusion.24 = bf16[128,48,384]{0,2,1:T(8,128)(2,1)} fusion(f32[48,384]{1,0:T(8,128)S(1)} %get-tuple-element.20, f32[48,384,128]{2,1,0:T(8,128)S(1)} %fusion.31, bf16[128,128]{1,0:T(8,128)(2,1)S(1)} %copy-done.16, bf16[1,48,384,128]{3,2,1,0:T(8,128)(2,1)S(1)} %bitcast.128, f32[128]{0:T(128)S(1)} %copy-done.11, f32[48,384]{1,0:T(8,128)S(1)} %get-tuple-element.19, ...), kind=kOutput, calls=%fused_computation.42 | convolution fusion | flops 629932032 | bytes 19128832 | tf_op jit(solution)/shard_map/rkd,dc->crk/dot_general | solution.py:43
  31.7 7.2 %copy.51 = bf16[128,48,384]{2,1,0:T(8,128)(2,1)} copy(bf16[128,48,384]{0,2,1:T(8,128)(2,1)} %fusion.24) | data formatting | bytes 9437184 | tf_op jit(solution)/shard_map/convert_element_type | solution.py:49
  38.9 7.4 %all-to-all-start.1 = ((bf16[128,48,384]{2,1,0:T(8,128)(2,1)}), bf16[128,48,384]{2,1,0:T(8,128)(2,1)}, u32[]{:S(2)}, u32[]{:S(2)}) async-start(bf16[128,48,384]{2,1,0:T(8,128)(2,1)} %copy.51), calls=%async_computation.1 | async-start | bytes 9437184 | tf_op jit(solution)/shard_map/all_to_all | solution.py:55
  46.3 9.5 %fusion.34 = f32[48,384,128]{2,1,0:T(8,128)S(1)} fusion(bf16[128,128]{1,0:T(8,128)(2,1)S(1)} %copy-done.7, bf16[1,48,384,128]{3,2,1,0:T(8,128)(2,1)} %param.13, f32[128]{0:T(128)S(1)} %copy-done.11, f32[48,384]{1,0:T(8,128)S(1)} %get-tuple-element.19, f32[48,384]{1,0:T(8,128)S(1)} %broadcast_multiply_fusion.2), kind=kOutput, calls=%fused_computation.61 | convolution fusion | flops 615776256 | bytes 14336512 | tf_op jit(solution)/shard_map/rkd,dc->crk/dot_general | solution.py:47
  55.8 10.6 %fusion.23 = bf16[128,48,384]{0,2,1:T(8,128)(2,1)} fusion(f32[48,384]{1,0:T(8,128)S(1)} %get-tuple-element.20, f32[48,384,128]{2,1,0:T(8,128)S(1)} %fusion.34, bf16[128,128]{1,0:T(8,128)(2,1)S(1)} %copy-done.17, bf16[1,48,384,128]{3,2,1,0:T(8,128)(2,1)S(1)} %bitcast.130, f32[128]{0:T(128)S(1)} %copy-done.11, f32[48,384]{1,0:T(8,128)S(1)} %get-tuple-element.19, ...), kind=kOutput, calls=%fused_computation.41 | convolution fusion | flops 629932032 | bytes 19128832 | tf_op jit(solution)/shard_map/rkd,dc->crk/dot_general | solution.py:43
  66.4 7.0 %copy.49 = bf16[128,48,384]{2,1,0:T(8,128)(2,1)} copy(bf16[128,48,384]{0,2,1:T(8,128)(2,1)} %fusion.23) | data formatting | bytes 9437184 | tf_op jit(solution)/shard_map/convert_element_type | solution.py:49
  73.3 77.5 %all-to-all-done.1 = bf16[128,48,384]{2,1,0:T(8,128)(2,1)} async-done(((bf16[128,48,384]{2,1,0:T(8,128)(2,1)}), bf16[128,48,384]{2,1,0:T(8,128)(2,1)}, u32[]{:S(2)}, u32[]{:S(2)}) %all-to-all-start.1) | async-done | bytes 4718624 | tf_op jit(solution)/shard_map/all_to_all | solution.py:55
  150.8 4.6 all-to-all-start
  155.4 5.2 copy.52
  160.6 98.5 %all-to-all-done = bf16[128,48,384]{2,1,0:T(8,128)(2,1)} async-done(((bf16[128,48,384]{2,1,0:T(8,128)(2,1)}), bf16[128,48,384]{2,1,0:T(8,128)(2,1)}, u32[]{:S(2)}, u32[]{:S(2)}) %all-to-all-start) | async-done | bytes 4718624 | tf_op jit(solution)/shard_map/all_to_all | solution.py:54
  259.1 3.2 copy.50
  262.3 0.5 copy-done.3
  262.9 3.4 convolution_convert_fusion
  266.3 5.0 copy.53
  271.3 4.7 all-to-all-start.2
  276.2 0.8 reshape.111
  277.0 102.7 %all-to-all-done.2 = bf16[16,384,384]{2,0,1:T(8,128)(2,1)} async-done(((bf16[16,384,384]{2,0,1:T(8,128)(2,1)}), bf16[16,384,384]{2,0,1:T(8,128)(2,1)}, u32[]{:S(2)}, u32[]{:S(2)}) %all-to-all-start.2) | async-done | bytes 4718624 | tf_op jit(solution)/shard_map/all_to_all | solution.py:60
  379.8 3.6 all-to-all-start.4
  383.4 3.5 copy.54
  386.9 0.7 fusion.12
  387.6 1.0 convert_bitcast_fusion.1
  388.6 1.3 multiply_reduce_fusion
  390.0 4.5 copy.55
  394.5 5.0 fusion.11
  399.6 1.5 fusion.21
  401.1 9.3 %fusion.7 = bf16[48,384,128]{2,1,0:T(8,128)(2,1)S(1)} fusion(bf16[1,48,384,128]{3,2,1,0:T(8,128)(2,1)S(1)} %bitcast.132, f32[48,384,128]{2,1,0:T(8,128)S(1)} %fusion.21, bf16[128,128]{1,0:T(8,128)(2,1)S(1)} %copy-done.18, f32[128]{0:T(128)S(1)} %copy-done.11, f32[48,384]{1,0:T(8,128)S(1)} %get-tuple-element.19, f32[48,384]{1,0:T(8,128)S(1)} %broadcast_multiply_fusion.2), kind=kOutput, calls=%fused_computation.9 | convolution fusion | flops 632291328 | bytes 19055104 | tf_op jit(solution)/shard_map/rkd,de->rke/dot_general | solution.py:66
  410.4 2.2 copy-done.4
  412.6 5.2 copy.57
  417.8 6.1 %all-to-all-start.3 = ((bf16[48,384,128]{2,0,1:T(8,128)(2,1)}), bf16[48,384,128]{2,0,1:T(8,128)(2,1)}, u32[]{:S(2)}, u32[]{:S(2)}) async-start(bf16[48,384,128]{2,0,1:T(8,128)(2,1)} %copy.57), calls=%async_computation.3 | async-start | bytes 9437184 | tf_op jit(solution)/shard_map/all_to_all | solution.py:70
  424.0 0.5 broadcast.101
  424.6 0.8 reduce.5
  425.6 102.4 %all-to-all-done.3 = bf16[48,384,128]{2,0,1:T(8,128)(2,1)} async-done(((bf16[48,384,128]{2,0,1:T(8,128)(2,1)}), bf16[48,384,128]{2,0,1:T(8,128)(2,1)}, u32[]{:S(2)}, u32[]{:S(2)}) %all-to-all-start.3) | async-done | bytes 4718624 | tf_op jit(solution)/shard_map/all_to_all | solution.py:70
  528.1 7.4 %copy.58 = f32[48,8,48,128]{3,0,1,2:T(8,128)} copy(bf16[48,8,48,128]{3,0,2,1:T(8,128)(2,1)} %bitcast.37) | data formatting | bytes 14155776 | tf_op jit(solution)/shard_map/convert_element_type | solution.py:72
  535.4 5.4 fusion.8
  540.9 1.8 bitcast_reduce_fusion
  542.7 2.2 fusion.20
  544.9 0.7 multiply_reduce_fusion.1
  545.6 3.9 convert_reduce_fusion.1
  549.5 1.0 convolution_bitcast_fusion
  550.5 38.4 %all-reduce = (f32[128,64]{0,1:T(8,128)S(1)}, f32[]{:T(128)}, f32[64]{0:T(128)S(1)}, f32[]{:T(128)}) all-reduce(f32[128,64]{0,1:T(8,128)S(1)} %convolution_bitcast_fusion, f32[]{:T(128)} %get-tuple-element.8, f32[64]{0:T(128)S(1)} %get-tuple-element.13, f32[]{:T(128)} %get-tuple-element.7), channel_id=1, replica_groups=mesh['res'=8,'rep'=4] {'res','rep'}, use_global_device_ids=true, to_apply=%region_6.0 | all-reduce | flops 8258 | bytes 66064 | tf_op jit(solution)/shard_map/psum | solution.py:95
  590.2 1.2 broadcast_divide_fusion.1
  591.4 1.3 broadcast_divide_fusion
  592.7 5.3 convert_bitcast_fusion.2
  (67 shorter events, 0.8 us)
Async XLA Ops:
  0.6 10.9 %copy-start = (bf16[128,128]{1,0:T(8,128)(2,1)S(1)}, bf16[128,128]{1,0:T(8,128)(2,1)}, u32[]{:S(2)}) copy-start(bf16[128,128]{1,0:T(8,128)(2,1)} %param.20) | copy-start | bytes 98308
  2.0 9.4 %copy-start.9 = (f32[384]{0:T(512)}, f32[384]{0:T(512)S(1)}, u32[]{:S(2)}) copy-start(f32[384]{0:T(512)S(1)} %convert_reduce_fusion.2) | copy-start | bytes 4612
  2.0 3.8 copy-start.2
  2.1 9.5 %copy-start.11 = (f32[128]{0:T(128)S(1)}, f32[128]{0:T(128)}, u32[]{:S(2)}) copy-start(f32[128]{0:T(128)} %param.16) | copy-start | bytes 1540
  5.9 15.2 %slice-start = ((s8[4718592]{0:T(1024)(128)(4,1)}), s8[524288]{0:T(1024)(128)(4,1)S(1)}, s32[]{:S(2)}) async-start(s8[4718592]{0:T(1024)(128)(4,1)} %bitcast.127), calls=%async_computation.5 | async-start | bytes 1048576
  11.5 9.6 %copy-start.13 = (f32[48]{0:T(128)}, f32[48]{0:T(128)S(1)}, u32[]{:S(2)}) copy-start(f32[48]{0:T(128)S(1)} %dynamic-slice_bitcast_fusion) | copy-start | bytes 580
  11.6 9.5 %slice-start.1 = ((s8[4718592]{0:T(1024)(128)(4,1)}), s8[4194304]{0:T(1024)(128)(4,1)S(1)}, s32[]{:S(2)}) async-start(s8[4718592]{0:T(1024)(128)(4,1)} %bitcast.127), calls=%async_computation.6 | async-start | bytes 8388608
  11.6 9.5 %copy-start.16 = (bf16[128,128]{1,0:T(8,128)(2,1)S(1)}, bf16[128,128]{1,0:T(8,128)(2,1)}, u32[]{:S(2)}) copy-start(bf16[128,128]{1,0:T(8,128)(2,1)} %param.19) | copy-start | bytes 98308
  38.9 7.4 %copy-start.7 = (bf16[128,128]{1,0:T(8,128)(2,1)S(1)}, bf16[128,128]{1,0:T(8,128)(2,1)}, u32[]{:S(2)}) copy-start(bf16[128,128]{1,0:T(8,128)(2,1)} %param.18) | copy-start | bytes 98308
  38.9 16.9 %slice-start.2 = ((s8[4718592]{0:T(1024)(128)(4,1)}), s8[524288]{0:T(1024)(128)(4,1)S(1)}, s32[]{:S(2)}) async-start(s8[4718592]{0:T(1024)(128)(4,1)} %bitcast.129), calls=%async_computation.7 | async-start | bytes 1048576
  38.9 111.9 %all-to-all-start.1 = ((bf16[128,48,384]{2,1,0:T(8,128)(2,1)}), bf16[128,48,384]{2,1,0:T(8,128)(2,1)}, u32[]{:S(2)}, u32[]{:S(2)}) async-start(bf16[128,48,384]{2,1,0:T(8,128)(2,1)} %copy.51), calls=%async_computation.1 | async-start | bytes 9437184 | tf_op jit(solution)/shard_map/all_to_all | solution.py:55
  46.3 9.5 %slice-start.3 = ((s8[4718592]{0:T(1024)(128)(4,1)}), s8[4194304]{0:T(1024)(128)(4,1)S(1)}, s32[]{:S(2)}) async-start(s8[4718592]{0:T(1024)(128)(4,1)} %bitcast.129), calls=%async_computation.8 | async-start | bytes 8388608
  46.3 9.5 %copy-start.17 = (bf16[128,128]{1,0:T(8,128)(2,1)S(1)}, bf16[128,128]{1,0:T(8,128)(2,1)}, u32[]{:S(2)}) copy-start(bf16[128,128]{1,0:T(8,128)(2,1)} %param.17) | copy-start | bytes 98308
  150.8 108.3 %all-to-all-start = ((bf16[128,48,384]{2,1,0:T(8,128)(2,1)}), bf16[128,48,384]{2,1,0:T(8,128)(2,1)}, u32[]{:S(2)}, u32[]{:S(2)}) async-start(bf16[128,48,384]{2,1,0:T(8,128)(2,1)} %copy.49), calls=%async_computation | async-start | bytes 9437184 | tf_op jit(solution)/shard_map/all_to_all | solution.py:54
  259.1 3.8 copy-start.3
  271.3 4.7 copy-start.5
  271.3 108.5 %all-to-all-start.2 = ((bf16[16,384,384]{2,0,1:T(8,128)(2,1)}), bf16[16,384,384]{2,0,1:T(8,128)(2,1)}, u32[]{:S(2)}, u32[]{:S(2)}) async-start(bf16[16,384,384]{2,0,1:T(8,128)(2,1)} %copy.53), calls=%async_computation.2 | async-start | bytes 9437184 | tf_op jit(solution)/shard_map/all_to_all | solution.py:60
  379.8 38.0 %all-to-all-start.4 = ((s32[8,1,2304]{2,1,0:T(1,128)}), s32[8,1,2304]{2,1,0:T(1,128)S(1)}, u32[]{:S(2)}, u32[]{:S(2)}) async-start(s32[8,1,2304]{2,1,0:T(1,128)} %reshape.111), calls=%async_computation.4 | async-start | bytes 147456 | tf_op jit(solution)/shard_map/all_to_all | solution.py:39
  389.9 4.6 copy-start.15
  390.0 11.1 %slice-start.4 = ((s8[4718592]{0:T(1024)(128)(4,1)}), s8[4194304]{0:T(1024)(128)(4,1)S(1)}, s32[]{:S(2)}) async-start(s8[4718592]{0:T(1024)(128)(4,1)} %bitcast.131), calls=%async_computation.9 | async-start | bytes 8388608
  394.5 5.0 copy-start.8
  394.5 6.5 %slice-start.5 = ((s8[4718592]{0:T(1024)(128)(4,1)}), s8[524288]{0:T(1024)(128)(4,1)S(1)}, s32[]{:S(2)}) async-start(s8[4718592]{0:T(1024)(128)(4,1)} %bitcast.131), calls=%async_computation.10 | async-start | bytes 1048576
  399.6 1.5 copy-start.18
  410.4 2.2 copy-start.4
  417.8 6.1 %copy-start.6 = (bf16[128,64]{0,1:T(8,128)(2,1)S(1)}, bf16[128,64]{0,1:T(8,128)(2,1)}, u32[]{:S(2)}) copy-start(bf16[128,64]{0,1:T(8,128)(2,1)} %param.24) | copy-start | bytes 49156
  417.8 110.3 %all-to-all-start.3 = ((bf16[48,384,128]{2,0,1:T(8,128)(2,1)}), bf16[48,384,128]{2,0,1:T(8,128)(2,1)}, u32[]{:S(2)}, u32[]{:S(2)}) async-start(bf16[48,384,128]{2,0,1:T(8,128)(2,1)} %copy.57), calls=%async_computation.3 | async-start | bytes 9437184 | tf_op jit(solution)/shard_map/all_to_all | solution.py:70
  425.5 109.9 %slice-start.6 = ((s8[4718592]{0:T(1024)(128)(4,1)}), s8[524288]{0:T(1024)(128)(4,1)S(1)}, s32[]{:S(2)}) async-start(s8[4718592]{0:T(1024)(128)(4,1)} %bitcast.139), calls=%async_computation.11 | async-start | bytes 1048576
  528.1 7.4 %slice-start.7 = ((s8[4718592]{0:T(1024)(128)(4,1)}), s8[4194304]{0:T(1024)(128)(4,1)S(1)}, s32[]{:S(2)}) async-start(s8[4718592]{0:T(1024)(128)(4,1)} %bitcast.139), calls=%async_computation.12 | async-start | bytes 8388608
  535.4 5.4 copy-start.12
  542.6 2.2 copy-start.10
  542.7 2.2 copy-start.14
  592.7 5.3 copy-start.1

commit v2 on v1

--- a/solution.py
+++ b/solution.py
@@ -2,6 +2,8 @@
 import jax.numpy as jnp
 from jax import lax
 from jax.sharding import PartitionSpec as P
+
+CHUNKS = 2
 
 
 def layer_norm(values, reduce_axis):
@@ -39,6 +41,17 @@
         lax.all_to_all(targets, "res", split_axis=1, concat_axis=0, tiled=True), 0, 1
     )
 
+    device_count = lax.axis_size("res")
+    group = device_count // 2
+    half_columns = crop_pair.shape[1] // 2
+    me = lax.axis_index("res")
+    half = me // group
+    place = me % group
+    groups = [list(range(group)), list(range(group, device_count))]
+    across = [(d, (d + group) % device_count) for d in range(device_count)]
+    own_start = half * half_columns
+    other_start = (1 - half) * half_columns
+
     def factor(project_weight, gating_weight):
         projected = jnp.einsum(
             "rkd,dc->crk", normed, project_weight, preferred_element_type=jnp.float32
@@ -48,27 +61,67 @@
         )
         return (gated * projected * pair_mask[None]).astype(jnp.bfloat16)
 
-    left_factor = factor(left_proj, left_gate)
-    right_factor = factor(right_proj, right_gate)
-    left_units, right_units = (
-        lax.all_to_all(left_factor, "res", split_axis=0, concat_axis=1, tiled=True),
-        lax.all_to_all(right_factor, "res", split_axis=0, concat_axis=1, tiled=True),
+    def in_half(values, split_axis, concat_axis):
+        return lax.all_to_all(
+            values,
+            "res",
+            split_axis=split_axis,
+            concat_axis=concat_axis,
+            axis_index_groups=groups,
+            tiled=True,
+        )
+
+    unit_chunk = left_proj.shape[1] // CHUNKS
+    spans = [slice(t * unit_chunk, (t + 1) * unit_chunk) for t in range(CHUNKS)]
+    right_own = [in_half(factor(right_proj[:, t], right_gate[:, t]), 0, 1) for t in spans]
+    right_other = [lax.ppermute(block, "res", across) for block in right_own]
+    left_own = [in_half(factor(left_proj[:, t], left_gate[:, t]), 0, 1) for t in spans]
+    gating = lax.optimization_barrier(
+        jax.nn.sigmoid(
+            jnp.einsum("rkd,de->rke", normed, gate_weight, preferred_element_type=jnp.float32)
+        )
     )
-    by_units = jnp.einsum(
-        "cik,cjk->cij", left_units, right_units, preferred_element_type=jnp.float32
-    ).astype(jnp.bfloat16)
-    triangle_out = lax.all_to_all(by_units, "res", split_axis=1, concat_axis=0, tiled=True)
-    normed_tri = (layer_norm(triangle_out.astype(jnp.float32), 0) * gain_out[:, None, None]).astype(
-        jnp.bfloat16
+
+    def updated_columns(right_blocks, start):
+        parts = []
+        for left_block, right_block in zip(left_own, right_blocks):
+            product = jnp.einsum(
+                "cik,cjk->cij", left_block, right_block, preferred_element_type=jnp.float32
+            ).astype(jnp.bfloat16)
+            parts.append(in_half(product, 1, 0))
+        triangle_out = jnp.concatenate(parts, axis=0)
+        normed_tri = (
+            layer_norm(triangle_out.astype(jnp.float32), 0) * gain_out[:, None, None]
+        ).astype(jnp.bfloat16)
+        update = jnp.einsum(
+            "crk,cd->rkd", normed_tri, out_weight, preferred_element_type=jnp.float32
+        )
+        gate_columns = lax.dynamic_slice_in_dim(gating, start, half_columns, 1)
+        pair_columns = lax.dynamic_slice_in_dim(crop_pair, start, half_columns, 1)
+        return (pair_columns.astype(jnp.float32) + gate_columns * update).astype(jnp.bfloat16)
+
+    updated_own = updated_columns(right_own, own_start)
+    mirrored = jnp.zeros((crop_pair.shape[1], row_count, crop_pair.shape[2]), jnp.bfloat16)
+    mirrored = lax.dynamic_update_slice_in_dim(
+        mirrored, in_half(updated_own, 1, 0), own_start, 0
     )
-    update = jnp.einsum("crk,cd->rkd", normed_tri, out_weight, preferred_element_type=jnp.float32)
-    gating = jax.nn.sigmoid(
-        jnp.einsum("rkd,de->rke", normed, gate_weight, preferred_element_type=jnp.float32)
-    )
-    updated = (pair_float + gating * update).astype(jnp.bfloat16)
-    mirrored = jnp.swapaxes(
-        lax.all_to_all(updated, "res", split_axis=1, concat_axis=0, tiled=True), 0, 1
-    )
+    updated_other = updated_columns(right_other, other_start)
+    for shift in range(group):
+        target = (place + shift) % group
+        source = (place - shift) % group
+        moves = [
+            (d, (1 - d // group) * group + (d % group + shift) % group)
+            for d in range(device_count)
+        ]
+        block = lax.dynamic_slice_in_dim(updated_other, target * row_count, row_count, 1)
+        arrived = lax.ppermute(block, "res", moves)
+        mirrored = lax.dynamic_update_slice_in_dim(
+            mirrored, arrived, other_start + source * row_count, 0
+        )
+    updated = jnp.zeros_like(crop_pair)
+    updated = lax.dynamic_update_slice_in_dim(updated, updated_own, own_start, 1)
+    updated = lax.dynamic_update_slice_in_dim(updated, updated_other, other_start, 1)
+    mirrored = jnp.swapaxes(mirrored, 0, 1)
     symmetric = (updated.astype(jnp.float32) + mirrored.astype(jnp.float32)).astype(jnp.bfloat16)
     logits = (
         jnp.einsum("rkd,dn->nrk", symmetric, head_weight, preferred_element_type=jnp.float32)

time: 601 us -> 636 us (1.058)
  waiting for transfers between devices: 381 us -> 314 us
  matrix products: 62.4 us -> 117 us
  starting transfers between devices: 26.5 us -> 71.1 us
    all_to_all x4 -> x9, waiting for transfers between devices: 381 us -> 98.2 us  [in_half(): lax.all_to_all(values, 'res', split_axis=split_axis, concat_axis=concat_a...]
    ppermute x0 -> x6, waiting for transfers between devices: none -> 216 us  [the longest x2 153 us: body(): right_other = [lax.ppermute(block, 'res', across) for block in right_own]]
    all_to_all x4 -> x9, starting transfers between devices: 22.9 us -> 52.5 us  [in_half(): lax.all_to_all(values, 'res', split_axis=split_axis, concat_axis=concat_a...]
    dot_general x2 -> x4, matrix products: 18.9 us -> 40.8 us  [factor(): jnp.einsum('rkd,dc->crk', normed, gating_weight, preferred_element_type=j...]
    dot_general x2 -> x4, matrix products: 21.1 us -> 37.1 us  [factor(): jnp.einsum('rkd,dc->crk', normed, project_weight, preferred_element_type=...]
    dot_general x2 -> x6, matrix products: 4.87 us -> 18.7 us  [the longest x4 9.69 us: updated_columns(): jnp.einsum('cik,cjk->cij', left_block, right_block, preferred_element_typ...]
    ppermute x0 -> x6, starting transfers between devices: none -> 12.1 us  [the longest x4 9.28 us: body(): arrived = lax.ppermute(block, 'res', moves)]
    convert_element_type x4 -> x5, local copies, waits for them, and re-layouts: 22.1 us -> 11.1 us  [the longest x4 8.11 us: updated_columns(): product = jnp.einsum('cik,cjk->cij', left_block, right_block, preferred_e...]
  transfers between devices with their start and end apart: 5 -> 16, of which waited for: 4 -> 12; matrix products, arithmetic and copies ran while one was open for 11% -> 23% of each run, Pallas kernels for 0% -> 0%
where the time goes in v2:
time: 636 us; the launch traced here: 633 us
  waiting for transfers between devices  314 us (49%)
  matrix products  117 us (18%)
  starting transfers between devices  71.1 us (11%)
  local copies, waits for them, and re-layouts  53.4 us (8%)
  blocking collectives  39.9 us (6%)
  other arithmetic  33.5 us (5%)
    ppermute x2, waiting for transfers between devices, body(): right_other = [lax.ppermute(block, 'res', across) for block in right_own]  153 us
    all_to_all x9, waiting for transfers between devices, in_half(): lax.all_to_all(values, 'res', split_axis=split_axis, concat_axis=concat_a...  98.2 us
    ppermute x4, waiting for transfers between devices, body(): arrived = lax.ppermute(block, 'res', moves)  62.9 us
    all_to_all x9, starting transfers between devices, in_half(): lax.all_to_all(values, 'res', split_axis=split_axis, concat_axis=concat_a...  52.5 us
    dot_general x4, matrix products, factor(): jnp.einsum('rkd,dc->crk', normed, gating_weight, preferred_element_type=j...  40.8 us
    psum x1, blocking collectives, body(): lax.psum((head_part, bias_part, loss_part, count_part), ('res', 'rep'))  39.9 us
    dot_general x4, matrix products, factor(): jnp.einsum('rkd,dc->crk', normed, project_weight, preferred_element_type=...  37.1 us
    all_to_all x9, local copies, waits for them, and re-layouts, in_half(): lax.all_to_all(values, 'res', split_axis=split_axis, concat_axis=concat_a...  19.3 us
  transfers between devices with their start and end apart: 16, of which 12 were waited for; matrix products, arithmetic and copies ran while one was open for 23% of the time, Pallas kernels for 0%

profile of v2, /device:TPU:0, one launch (start us, length us, event | category | flops | bytes accessed | tf_op | source)
XLA Modules:
  0.0 632.9 jit_solution(1816247274953327654)
XLA Ops:
  2.1 3.8 convert_reduce_fusion
  5.9 5.5 fusion.3
  11.6 10.0 %fusion.57 = f32[48,384,64]{1,2,0:T(8,128)S(1)} fusion(bf16[128,128]{1,0:T(8,128)(2,1)S(1)} %copy-done.9, bf16[1,48,384,128]{3,2,1,0:T(8,128)(2,1)} %param.13, f32[128]{0:T(128)S(1)} %copy-done.11, f32[48,384]{1,0:T(8,128)S(1)} %get-tuple-element.29, f32[48,384]{1,0:T(8,128)S(1)} %broadcast_multiply_fusion.1), kind=kOutput, calls=%fused_computation.90 | convolution fusion | flops 313786368 | bytes 9617920 | tf_op jit(solution)/shard_map/rkd,dc->crk/dot_general | solution.py:60
  21.6 9.0 %fusion.34 = bf16[64,48,384]{2,0,1:T(8,128)(2,1)S(1)} fusion(f32[48,384]{1,0:T(8,128)S(1)} %get-tuple-element.30, f32[48,384,64]{1,2,0:T(8,128)S(1)} %fusion.57, bf16[128,128]{1,0:T(8,128)(2,1)S(1)} %copy-done.15, bf16[1,48,384,128]{3,2,1,0:T(8,128)(2,1)S(1)} %bitcast.180, f32[128]{0:T(128)S(1)} %copy-done.11, f32[48,384]{1,0:T(8,128)S(1)} %get-tuple-element.29, ...), kind=kOutput, calls=%fused_computation.58 | convolution fusion | flops 320864256 | bytes 12050944 | tf_op jit(solution)/shard_map/rkd,dc->crk/dot_general | solution.py:56
  30.6 2.8 copy.108
  33.4 5.4 all-to-all-start.1
  38.8 10.0 %fusion.60 = f32[48,384,64]{1,2,0:T(8,128)S(1)} fusion(bf16[128,128]{1,0:T(8,128)(2,1)S(1)} %copy-done.8, bf16[1,48,384,128]{3,2,1,0:T(8,128)(2,1)} %param.13, f32[128]{0:T(128)S(1)} %copy-done.11, f32[48,384]{1,0:T(8,128)S(1)} %get-tuple-element.29, f32[48,384]{1,0:T(8,128)S(1)} %broadcast_multiply_fusion.1), kind=kOutput, calls=%fused_computation.93 | convolution fusion | flops 313786368 | bytes 9617920 | tf_op jit(solution)/shard_map/rkd,dc->crk/dot_general | solution.py:60
  48.8 9.0 %fusion.33 = bf16[64,48,384]{2,0,1:T(8,128)(2,1)S(1)} fusion(f32[48,384]{1,0:T(8,128)S(1)} %get-tuple-element.30, f32[48,384,64]{1,2,0:T(8,128)S(1)} %fusion.60, bf16[128,128]{1,0:T(8,128)(2,1)S(1)} %copy-done.14, bf16[1,48,384,128]{3,2,1,0:T(8,128)(2,1)S(1)} %bitcast.182, f32[128]{0:T(128)S(1)} %copy-done.11, f32[48,384]{1,0:T(8,128)S(1)} %get-tuple-element.29, ...), kind=kOutput, calls=%fused_computation.57 | convolution fusion | flops 320864256 | bytes 12050944 | tf_op jit(solution)/shard_map/rkd,dc->crk/dot_general | solution.py:56
  57.8 2.8 copy.104
  60.6 5.8 all-to-all-done.1
  66.5 4.6 all-to-all-start
  71.1 10.4 %fusion.54 = f32[48,384,64]{1,2,0:T(8,128)S(1)} fusion(bf16[128,128]{1,0:T(8,128)(2,1)S(1)} %copy-done.8, bf16[1,48,384,128]{3,2,1,0:T(8,128)(2,1)} %param.13, f32[128]{0:T(128)S(1)} %copy-done.11, f32[48,384]{1,0:T(8,128)S(1)} %get-tuple-element.29, f32[48,384]{1,0:T(8,128)S(1)} %broadcast_multiply_fusion.1), kind=kOutput, calls=%fused_computation.87 | convolution fusion | flops 313786368 | bytes 9617920 | tf_op jit(solution)/shard_map/rkd,dc->crk/dot_general | solution.py:60
  81.6 9.6 %fusion.35 = bf16[64,48,384]{2,0,1:T(8,128)(2,1)S(1)} fusion(f32[48,384]{1,0:T(8,128)S(1)} %get-tuple-element.30, f32[48,384,64]{1,2,0:T(8,128)S(1)} %fusion.54, bf16[128,128]{1,0:T(8,128)(2,1)S(1)} %copy-done.14, bf16[1,48,384,128]{3,2,1,0:T(8,128)(2,1)S(1)} %bitcast.184, f32[128]{0:T(128)S(1)} %copy-done.11, f32[48,384]{1,0:T(8,128)S(1)} %get-tuple-element.29, ...), kind=kOutput, calls=%fused_computation.59 | convolution fusion | flops 320864256 | bytes 12050944 | tf_op jit(solution)/shard_map/rkd,dc->crk/dot_general | solution.py:56
  91.1 2.8 copy.115
  93.9 5.1 all-to-all-done
  99.0 16.0 %all-to-all-start.3 = ((bf16[64,48,384]{2,1,0:T(8,128)(2,1)}), bf16[64,48,384]{2,1,0:T(8,128)(2,1)}, u32[]{:S(2)}, u32[]{:S(2)}) async-start(bf16[64,48,384]{2,1,0:T(8,128)(2,1)} %copy.115), calls=%async_computation.3 | async-start | bytes 4718592 | tf_op jit(solution)/shard_map/all_to_all | solution.py:65
  115.0 10.4 %fusion.51 = f32[48,384,64]{1,2,0:T(8,128)S(1)} fusion(bf16[128,128]{1,0:T(8,128)(2,1)S(1)} %copy-done.9, bf16[1,48,384,128]{3,2,1,0:T(8,128)(2,1)} %param.13, f32[128]{0:T(128)S(1)} %copy-done.11, f32[48,384]{1,0:T(8,128)S(1)} %get-tuple-element.29, f32[48,384]{1,0:T(8,128)S(1)} %broadcast_multiply_fusion.1), kind=kOutput, calls=%fused_computation.84 | convolution fusion | flops 313786368 | bytes 9617920 | tf_op jit(solution)/shard_map/rkd,dc->crk/dot_general | solution.py:60
  125.5 9.6 %fusion.36 = bf16[64,48,384]{2,0,1:T(8,128)(2,1)S(1)} fusion(f32[48,384]{1,0:T(8,128)S(1)} %get-tuple-element.30, f32[48,384,64]{1,2,0:T(8,128)S(1)} %fusion.51, bf16[128,128]{1,0:T(8,128)(2,1)S(1)} %copy-done.15, bf16[1,48,384,128]{3,2,1,0:T(8,128)(2,1)S(1)} %bitcast.186, f32[128]{0:T(128)S(1)} %copy-done.11, f32[48,384]{1,0:T(8,128)S(1)} %get-tuple-element.29, ...), kind=kOutput, calls=%fused_computation.60 | convolution fusion | flops 320864256 | bytes 12050944 | tf_op jit(solution)/shard_map/rkd,dc->crk/dot_general | solution.py:56
  135.1 2.8 copy.119
  137.9 4.4 all-to-all-done.3
  142.2 4.5 all-to-all-start.4
  156.7 17.5 %all-to-all-done.4 = bf16[64,48,384]{2,1,0:T(8,128)(2,1)} async-done(((bf16[64,48,384]{2,1,0:T(8,128)(2,1)}), bf16[64,48,384]{2,1,0:T(8,128)(2,1)}, u32[]{:S(2)}, u32[]{:S(2)}) %all-to-all-start.4) | async-done | bytes 2359328 | tf_op jit(solution)/shard_map/all_to_all | solution.py:65
  174.2 4.4 all-to-all-start.2
  178.5 2.8 collective-permute-start
  189.8 26.2 %all-to-all-done.2 = bf16[16,192,192]{2,0,1:T(8,128)(2,1)} async-done(((bf16[16,192,192]{2,0,1:T(8,128)(2,1)}), bf16[16,192,192]{2,0,1:T(8,128)(2,1)}, u32[]{:S(2)}, u32[]{:S(2)}) %all-to-all-start.2) | async-done | bytes 1179680 | tf_op jit(solution)/shard_map/all_to_all | solution.py:65
  216.0 4.4 all-to-all-start.5
  220.5 114.7 %collective-permute-done = bf16[16,192,384]{2,1,0:T(8,128)(2,1)} collective-permute-done((bf16[16,192,384]{2,1,0:T(8,128)(2,1)}, bf16[16,192,384]{2,1,0:T(8,128)(2,1)}, u32[]{:S(2)}, u32[]{:S(2)}) %collective-permute-start) | collective-permute-done | bytes 2359328 | tf_op jit(solution)/shard_map/ppermute | solution.py:77
  335.1 3.4 convolution_convert_fusion.1
  340.5 4.4 all-to-all-start.6
  344.9 38.3 %collective-permute-done.1 = bf16[16,192,384]{2,1,0:T(8,128)(2,1)} collective-permute-done((bf16[16,192,384]{2,1,0:T(8,128)(2,1)}, bf16[16,192,384]{2,1,0:T(8,128)(2,1)}, u32[]{:S(2)}, u32[]{:S(2)}) %collective-permute-start.1) | collective-permute-done | bytes 2359328 | tf_op jit(solution)/shard_map/ppermute | solution.py:77
  387.9 12.1 %all-to-all-done.6 = bf16[16,192,192]{2,0,1:T(8,128)(2,1)} async-done(((bf16[16,192,192]{2,0,1:T(8,128)(2,1)}), bf16[16,192,192]{2,0,1:T(8,128)(2,1)}, u32[]{:S(2)}, u32[]{:S(2)}) %all-to-all-start.6) | async-done | bytes 1179680 | tf_op jit(solution)/shard_map/all_to_all | solution.py:65
  400.0 4.4 all-to-all-start.7
  404.4 11.0 %add_divide_fusion = f32[48,384,128]{2,1,0:T(8,128)} fusion(bf16[128,128]{1,0:T(8,128)(2,1)S(1)} %copy-done.16, bf16[1,48,384,128]{3,2,1,0:T(8,128)(2,1)} %param.13, f32[128]{0:T(128)S(1)} %copy-done.11, f32[48,384]{1,0:T(8,128)S(1)} %get-tuple-element.29, f32[48,384]{1,0:T(8,128)S(1)} %broadcast_multiply_fusion.1), kind=kOutput, calls=%fused_computation.10 | convolution fusion | flops 622854144 | bytes 14336512 | tf_op jit(solution)/shard_map/rkd,de->rke/dot_general | solution.py:81
  422.0 3.1 copy.127
  425.2 6.6 %all-to-all-start.9 = ((s32[8,1,2304]{2,1,0:T(1,128)}), s32[8,1,2304]{2,1,0:T(1,128)S(1)}, u32[]{:S(2)}, u32[]{:S(2)}) async-start(s32[8,1,2304]{2,1,0:T(1,128)} %reshape.120), calls=%async_computation.9 | async-start | bytes 147456 | tf_op jit(solution)/shard_map/all_to_all | solution.py:41
  437.3 7.5 %fusion.13 = (bf16[128,48,192]{2,1,0:T(8,128)(2,1)}, bf16[128,48,192]{2,1,0:T(8,128)(2,1)S(1)}) fusion(f32[48,192]{1,0:T(8,128)S(1)} %add_rsqrt_fusion.1, f32[48,192]{1,0:T(8,128)S(1)} %broadcast_multiply_fusion.2, f32[128]{0:T(128)S(1)} %copy-done.13, bf16[64,48,192]{2,1,0:T(8,128)(2,1)S(1)} %bitcast.203, bf16[64,48,192]{2,1,0:T(8,128)(2,1)S(1)} %bitcast.200, ...), kind=kLoop, calls=%fused_computation.21 | loop fusion | flops 14155776 | bytes 9585152 | tf_op jit(solution)/shard_map/convert_element_type | solution.py:95
  450.8 2.9 copy.132
  453.7 4.5 all-to-all-start.8
  458.4 6.4 %constant_dynamic-update-slice_fusion.1 = (bf16[48,384,128]{2,1,0:T(8,128)(2,1)}, bf16[48,192,128]{2,1,0:T(8,128)(2,1)S(1)}) fusion(bf16[48,384,128]{2,1,0:T(8,128)(2,1)} %copy-done.2, s32[]{:T(128)S(6)} %select_n.82, bf16[128,128]{1,0:T(8,128)(2,1)S(1)} %copy-done, bf16[128,48,192]{2,1,0:T(8,128)(2,1)S(1)} %copy-done.5, ...), kind=kOutput, calls=%fused_computation.115 | convolution fusion | flops 306708480 | bytes 14188548 | tf_op jit(solution)/shard_map/crk,cd->rkd/dot_general | solution.py:96
  466.2 2.9 collective-permute-start.2
  472.3 3.7 collective-permute-start.4
  477.2 27.2 %all-to-all-done.8 = bf16[48,192,128]{2,0,1:T(8,128)(2,1)} async-done(((bf16[48,192,128]{2,0,1:T(8,128)(2,1)}), bf16[48,192,128]{2,0,1:T(8,128)(2,1)}, u32[]{:S(2)}, u32[]{:S(2)}) %all-to-all-start.8) | async-done | bytes 2359328 | tf_op jit(solution)/shard_map/all_to_all | solution.py:65
  508.5 7.5 %collective-permute-done.3 = bf16[48,48,128]{2,1,0:T(8,128)(2,1)S(1)} collective-permute-done((bf16[48,48,128]{2,1,0:T(8,128)(2,1)}, bf16[48,48,128]{2,1,0:T(8,128)(2,1)S(1)}, u32[]{:S(2)}, u32[]{:S(2)}) %collective-permute-start.3) | collective-permute-done | bytes 589856 | tf_op jit(solution)/shard_map/ppermute | solution.py:117
  516.1 11.5 %collective-permute-done.4 = bf16[48,48,128]{2,1,0:T(8,128)(2,1)S(1)} collective-permute-done((bf16[48,48,128]{2,1,0:T(8,128)(2,1)}, bf16[48,48,128]{2,1,0:T(8,128)(2,1)S(1)}, u32[]{:S(2)}, u32[]{:S(2)}) %collective-permute-start.4) | collective-permute-done | bytes 589856 | tf_op jit(solution)/shard_map/ppermute | solution.py:117
  527.9 43.9 %collective-permute-done.5 = bf16[48,48,128]{2,1,0:T(8,128)(2,1)S(1)} collective-permute-done((bf16[48,48,128]{2,1,0:T(8,128)(2,1)S(1)}, bf16[48,48,128]{2,1,0:T(8,128)(2,1)S(1)}, u32[]{:S(2)}, u32[]{:S(2)}) %collective-permute-start.5) | collective-permute-done | bytes 589856 | tf_op jit(solution)/shard_map/ppermute | solution.py:117
  577.0 3.9 convert_reduce_fusion.3
  582.5 39.9 %all-reduce = (f32[128,64]{0,1:T(8,128)S(1)}, f32[]{:T(128)}, f32[64]{0:T(128)S(1)}, f32[]{:T(128)}) all-reduce(f32[128,64]{0,1:T(8,128)S(1)} %fusion.45, f32[]{:T(128)} %get-tuple-element.8, f32[64]{0:T(128)S(1)} %get-tuple-element.13, f32[]{:T(128)} %get-tuple-element.7), channel_id=1, replica_groups=mesh['res'=8,'rep'=4] {'res','rep'}, use_global_device_ids=true, to_apply=%region_8.9 | all-reduce | flops 8258 | bytes 66064 | tf_op jit(solution)/shard_map/psum | solution.py:148
  626.2 5.3 convert_bitcast_fusion.1
  (129 shorter events, 64.2 us)
Async XLA Ops:
  0.6 445.3 %copy-start = (bf16[128,128]{1,0:T(8,128)(2,1)S(1)}, bf16[128,128]{1,0:T(8,128)(2,1)}, u32[]{:S(2)}) copy-start(bf16[128,128]{1,0:T(8,128)(2,1)} %param.23) | copy-start | bytes 98308
  2.0 3.9 copy-start.1
  2.0 9.5 %copy-start.9 = (bf16[128,128]{1,0:T(8,128)(2,1)S(1)}, bf16[128,128]{1,0:T(8,128)(2,1)}, u32[]{:S(2)}) copy-start(bf16[128,128]{1,0:T(8,128)(2,1)} %param.20) | copy-start | bytes 98308
  2.1 9.5 %copy-start.11 = (f32[128]{0:T(128)S(1)}, f32[128]{0:T(128)}, u32[]{:S(2)}) copy-start(f32[128]{0:T(128)} %param.16) | copy-start | bytes 1540
  11.5 10.1 %slice-start = ((s8[4718592]{0:T(1024)(128)(4,1)}), s8[4194304]{0:T(1024)(128)(4,1)S(1)}, s32[]{:S(2)}) async-start(s8[4718592]{0:T(1024)(128)(4,1)} %bitcast.179), calls=%async_computation.10 | async-start | bytes 8388608
  11.6 10.0 %slice-start.1 = ((s8[4718592]{0:T(1024)(128)(4,1)}), s8[524288]{0:T(1024)(128)(4,1)S(1)}, s32[]{:S(2)}) async-start(s8[4718592]{0:T(1024)(128)(4,1)} %bitcast.179), calls=%async_computation.11 | async-start | bytes 1048576
  11.6 10.0 %copy-start.15 = (bf16[128,128]{1,0:T(8,128)(2,1)S(1)}, bf16[128,128]{1,0:T(8,128)(2,1)}, u32[]{:S(2)}) copy-start(bf16[128,128]{1,0:T(8,128)(2,1)} %param.19) | copy-start | bytes 98308
  30.6 8.2 %copy-start.8 = (bf16[128,128]{1,0:T(8,128)(2,1)S(1)}, bf16[128,128]{1,0:T(8,128)(2,1)}, u32[]{:S(2)}) copy-start(bf16[128,128]{1,0:T(8,128)(2,1)} %param.18) | copy-start | bytes 98308
  33.4 15.3 %slice-start.2 = ((s8[4718592]{0:T(1024)(128)(4,1)}), s8[524288]{0:T(1024)(128)(4,1)S(1)}, s32[]{:S(2)}) async-start(s8[4718592]{0:T(1024)(128)(4,1)} %bitcast.181), calls=%async_computation.12 | async-start | bytes 1048576
  33.4 33.0 %all-to-all-start.1 = ((bf16[64,48,384]{2,1,0:T(8,128)(2,1)}), bf16[64,48,384]{2,1,0:T(8,128)(2,1)S(1)}, u32[]{:S(2)}, u32[]{:S(2)}) async-start(bf16[64,48,384]{2,1,0:T(8,128)(2,1)} %copy.108), calls=%async_computation.1 | async-start | bytes 4718592 | tf_op jit(solution)/shard_map/all_to_all | solution.py:65
  38.8 10.0 %slice-start.3 = ((s8[4718592]{0:T(1024)(128)(4,1)}), s8[4194304]{0:T(1024)(128)(4,1)S(1)}, s32[]{:S(2)}) async-start(s8[4718592]{0:T(1024)(128)(4,1)} %bitcast.181), calls=%async_computation.13 | async-start | bytes 8388608
  38.8 10.0 %copy-start.14 = (bf16[128,128]{1,0:T(8,128)(2,1)S(1)}, bf16[128,128]{1,0:T(8,128)(2,1)}, u32[]{:S(2)}) copy-start(bf16[128,128]{1,0:T(8,128)(2,1)} %param.17) | copy-start | bytes 98308
  66.5 15.1 %slice-start.4 = ((s8[4718592]{0:T(1024)(128)(4,1)}), s8[524288]{0:T(1024)(128)(4,1)S(1)}, s32[]{:S(2)}) async-start(s8[4718592]{0:T(1024)(128)(4,1)} %bitcast.183), calls=%async_computation.14 | async-start | bytes 1048576
  66.5 32.5 %all-to-all-start = ((bf16[64,48,384]{2,1,0:T(8,128)(2,1)}), bf16[64,48,384]{2,1,0:T(8,128)(2,1)}, u32[]{:S(2)}, u32[]{:S(2)}) async-start(bf16[64,48,384]{2,1,0:T(8,128)(2,1)} %copy.104), calls=%async_computation | async-start | bytes 4718592 | tf_op jit(solution)/shard_map/all_to_all | solution.py:65
  71.1 10.5 %slice-start.5 = ((s8[4718592]{0:T(1024)(128)(4,1)}), s8[4194304]{0:T(1024)(128)(4,1)S(1)}, s32[]{:S(2)}) async-start(s8[4718592]{0:T(1024)(128)(4,1)} %bitcast.183), calls=%async_computation.15 | async-start | bytes 8388608
  99.0 26.5 %slice-start.6 = ((s8[4718592]{0:T(1024)(128)(4,1)}), s8[524288]{0:T(1024)(128)(4,1)S(1)}, s32[]{:S(2)}) async-start(s8[4718592]{0:T(1024)(128)(4,1)} %bitcast.185), calls=%async_computation.16 | async-start | bytes 1048576
  99.0 43.2 %all-to-all-start.3 = ((bf16[64,48,384]{2,1,0:T(8,128)(2,1)}), bf16[64,48,384]{2,1,0:T(8,128)(2,1)}, u32[]{:S(2)}, u32[]{:S(2)}) async-start(bf16[64,48,384]{2,1,0:T(8,128)(2,1)} %copy.115), calls=%async_computation.3 | async-start | bytes 4718592 | tf_op jit(solution)/shard_map/all_to_all | solution.py:65
  115.0 10.5 %slice-start.7 = ((s8[4718592]{0:T(1024)(128)(4,1)}), s8[4194304]{0:T(1024)(128)(4,1)S(1)}, s32[]{:S(2)}) async-start(s8[4718592]{0:T(1024)(128)(4,1)} %bitcast.185), calls=%async_computation.17 | async-start | bytes 8388608
  142.2 32.0 %all-to-all-start.4 = ((bf16[64,48,384]{2,1,0:T(8,128)(2,1)}), bf16[64,48,384]{2,1,0:T(8,128)(2,1)}, u32[]{:S(2)}, u32[]{:S(2)}) async-start(bf16[64,48,384]{2,1,0:T(8,128)(2,1)} %copy.119), calls=%async_computation.4 | async-start | bytes 4718592 | tf_op jit(solution)/shard_map/all_to_all | solution.py:65
  150.5 1.4 copy-start.4
  174.2 41.8 %all-to-all-start.2 = ((bf16[16,192,192]{2,0,1:T(8,128)(2,1)}), bf16[16,192,192]{2,0,1:T(8,128)(2,1)}, u32[]{:S(2)}, u32[]{:S(2)}) async-start(bf16[16,192,192]{2,0,1:T(8,128)(2,1)} %copy.110), calls=%async_computation.2 | async-start | bytes 3145728 | tf_op jit(solution)/shard_map/all_to_all | solution.py:65
  178.5 156.6 %collective-permute-start = (bf16[16,192,384]{2,1,0:T(8,128)(2,1)}, bf16[16,192,384]{2,1,0:T(8,128)(2,1)}, u32[]{:S(2)}, u32[]{:S(2)}) collective-permute-start(bf16[16,192,384]{2,1,0:T(8,128)(2,1)} %bitcast.15), channel_id=1, source_target_pairs={{0,16},{4,20},{8,24},{12,28},{16,0},{20,4},{24,8},{28,12},{1,17},{... | collective-permute-start | bytes 7077896 | tf_op jit(solution)/shard_map/ppermute | solution.py:77
  185.4 1.4 copy-start.6
  216.0 124.5 %all-to-all-start.5 = ((bf16[16,192,192]{2,0,1:T(8,128)(2,1)}), bf16[16,192,192]{2,0,1:T(8,128)(2,1)}, u32[]{:S(2)}, u32[]{:S(2)}) async-start(bf16[16,192,192]{2,0,1:T(8,128)(2,1)} %copy.121), calls=%async_computation.5 | async-start | bytes 3145728 | tf_op jit(solution)/shard_map/all_to_all | solution.py:65
  220.4 162.8 %collective-permute-start.1 = (bf16[16,192,384]{2,1,0:T(8,128)(2,1)}, bf16[16,192,384]{2,1,0:T(8,128)(2,1)}, u32[]{:S(2)}, u32[]{:S(2)}) collective-permute-start(bf16[16,192,384]{2,1,0:T(8,128)(2,1)} %bitcast.209), channel_id=1, source_target_pairs={{0,16},{4,20},{8,24},{12,28},{16,0},{20,4},{24,8},{28,12},{1,17},{... | collective-permute-start | bytes 7077896 | tf_op jit(solution)/shard_map/ppermute | solution.py:77
  340.5 59.4 %all-to-all-start.6 = ((bf16[16,192,192]{2,0,1:T(8,128)(2,1)}), bf16[16,192,192]{2,0,1:T(8,128)(2,1)}, u32[]{:S(2)}, u32[]{:S(2)}) async-start(bf16[16,192,192]{2,0,1:T(8,128)(2,1)} %copy.125), calls=%async_computation.6 | async-start | bytes 3145728 | tf_op jit(solution)/shard_map/all_to_all | solution.py:65
  385.9 18.5 %copy-start.16 = (bf16[128,128]{1,0:T(8,128)(2,1)S(1)}, bf16[128,128]{1,0:T(8,128)(2,1)}, u32[]{:S(2)}) copy-start(bf16[128,128]{1,0:T(8,128)(2,1)} %param.21) | copy-start | bytes 98308
  400.0 25.2 %all-to-all-start.7 = ((bf16[16,192,192]{2,0,1:T(8,128)(2,1)}), bf16[16,192,192]{2,0,1:T(8,128)(2,1)}, u32[]{:S(2)}, u32[]{:S(2)}) async-start(bf16[16,192,192]{2,0,1:T(8,128)(2,1)} %copy.128), calls=%async_computation.7 | async-start | bytes 3145728 | tf_op jit(solution)/shard_map/all_to_all | solution.py:65
  404.3 11.0 %copy-start.7 = (s32[1,48,384]{2,1,0:T(8,128)S(1)}, s32[1,48,384]{2,1,0:T(8,128)}, u32[]{:S(2)}) copy-start(s32[1,48,384]{2,1,0:T(8,128)} %param.15) | copy-start | bytes 221188
  425.2 28.6 %all-to-all-start.9 = ((s32[8,1,2304]{2,1,0:T(1,128)}), s32[8,1,2304]{2,1,0:T(1,128)S(1)}, u32[]{:S(2)}, u32[]{:S(2)}) async-start(s32[8,1,2304]{2,1,0:T(1,128)} %reshape.120), calls=%async_computation.9 | async-start | bytes 147456 | tf_op jit(solution)/shard_map/all_to_all | solution.py:41
  431.7 4.4 copy-start.3
  431.8 5.5 copy-start.13
  433.9 12.1 %slice-start.8 = ((s8[4718592]{0:T(1024)(128)(4,1)}), s8[4194304]{0:T(1024)(128)(4,1)S(1)}, s32[]{:S(2)}) async-start(s8[4718592]{0:T(1024)(128)(4,1)} %bitcast.187), calls=%async_computation.18 | async-start | bytes 8388608
  436.2 9.8 %slice-start.12 = ((s8[9437184]{0:T(1024)(128)(4,1)}), s8[4194304]{0:T(1024)(128)(4,1)S(1)}, s32[]{:S(2)}) async-start(s8[9437184]{0:T(1024)(128)(4,1)} %bitcast.212), calls=%async_computation.22 | async-start | bytes 8388608
  437.3 8.7 %slice-start.9 = ((s8[4718592]{0:T(1024)(128)(4,1)}), s8[524288]{0:T(1024)(128)(4,1)S(1)}, s32[]{:S(2)}) async-start(s8[4718592]{0:T(1024)(128)(4,1)} %bitcast.187), calls=%async_computation.19 | async-start | bytes 1048576
  437.3 8.7 %slice-start.13 = ((s8[9437184]{0:T(1024)(128)(4,1)}), s8[4194304]{0:T(1024)(128)(4,1)S(1)}, s32[]{:S(2)}) async-start(s8[9437184]{0:T(1024)(128)(4,1)} %bitcast.212), calls=%async_computation.23 | async-start | bytes 8388608
  437.3 8.7 %slice-start.14 = ((s8[9437184]{0:T(1024)(128)(4,1)}), s8[1048576]{0:T(1024)(128)(4,1)S(1)}, s32[]{:S(2)}) async-start(s8[9437184]{0:T(1024)(128)(4,1)} %bitcast.212), calls=%async_computation.24 | async-start | bytes 2097152
  448.6 2.2 copy-start.2
  450.8 7.6 %copy-start.5 = (bf16[128,48,192]{2,1,0:T(8,128)(2,1)S(1)}, bf16[128,48,192]{2,1,0:T(8,128)(2,1)}, u32[]{:S(2)}) copy-start(bf16[128,48,192]{2,1,0:T(8,128)(2,1)} %get-tuple-element.21) | copy-start | bytes 7077892
  453.7 50.7 %all-to-all-start.8 = ((bf16[48,192,128]{2,0,1:T(8,128)(2,1)}), bf16[48,192,128]{2,0,1:T(8,128)(2,1)}, u32[]{:S(2)}, u32[]{:S(2)}) async-start(bf16[48,192,128]{2,0,1:T(8,128)(2,1)} %copy.132), calls=%async_computation.8 | async-start | bytes 4718592 | tf_op jit(solution)/shard_map/all_to_all | solution.py:65
  464.8 5.8 copy-start.10
  466.2 42.1 %collective-permute-start.2 = (bf16[48,48,128]{2,1,0:T(8,128)(2,1)}, bf16[48,48,128]{2,1,0:T(8,128)(2,1)S(1)}, u32[]{:S(2)}, u32[]{:S(2)}) collective-permute-start(bf16[48,48,128]{2,1,0:T(8,128)(2,1)} %get-tuple-element.20), channel_id=1, source_target_pairs={{0,16},{4,20},{8,24},{12,28},{16,0},{20,4},{24,8},{28,12},{1,17},{... | collective-permute-start | bytes 1769480 | tf_op jit(solution)/shard_map/ppermute | solution.py:117
  469.1 46.8 %collective-permute-start.3 = (bf16[48,48,128]{2,1,0:T(8,128)(2,1)}, bf16[48,48,128]{2,1,0:T(8,128)(2,1)S(1)}, u32[]{:S(2)}, u32[]{:S(2)}) collective-permute-start(bf16[48,48,128]{2,1,0:T(8,128)(2,1)} %get-tuple-element.19), channel_id=1, source_target_pairs={{0,20},{4,24},{8,28},{12,16},{16,4},{20,8},{24,12},{28,0},{1,21},{... | collective-permute-start | bytes 1769480 | tf_op jit(solution)/shard_map/ppermute | solution.py:117
  472.3 55.4 %collective-permute-start.4 = (bf16[48,48,128]{2,1,0:T(8,128)(2,1)}, bf16[48,48,128]{2,1,0:T(8,128)(2,1)S(1)}, u32[]{:S(2)}, u32[]{:S(2)}) collective-permute-start(bf16[48,48,128]{2,1,0:T(8,128)(2,1)} %get-tuple-element.18), channel_id=1, source_target_pairs={{0,24},{4,28},{8,16},{12,20},{16,8},{20,12},{24,0},{28,4},{1,25},{... | collective-permute-start | bytes 1769480 | tf_op jit(solution)/shard_map/ppermute | solution.py:117
  476.0 95.7 %collective-permute-start.5 = (bf16[48,48,128]{2,1,0:T(8,128)(2,1)S(1)}, bf16[48,48,128]{2,1,0:T(8,128)(2,1)S(1)}, u32[]{:S(2)}, u32[]{:S(2)}) collective-permute-start(bf16[48,48,128]{2,1,0:T(8,128)(2,1)S(1)} %get-tuple-element.17), channel_id=1, source_target_pairs={{0,28},{4,16},{8,20},{12,24},{16,12},{20,0},{24,4},{28,8},{1,29},{... | collective-permute-start | bytes 1769480 | tf_op jit(solution)/shard_map/ppermute | solution.py:117
  506.8 65.2 %slice-start.10 = ((s8[4718592]{0:T(1024)(128)(4,1)}), s8[4194304]{0:T(1024)(128)(4,1)S(1)}, s32[]{:S(2)}) async-start(s8[4718592]{0:T(1024)(128)(4,1)} %bitcast.190), calls=%async_computation.20 | async-start | bytes 8388608
  507.9 64.1 %slice-start.11 = ((s8[4718592]{0:T(1024)(128)(4,1)}), s8[524288]{0:T(1024)(128)(4,1)S(1)}, s32[]{:S(2)}) async-start(s8[4718592]{0:T(1024)(128)(4,1)} %bitcast.190), calls=%async_computation.21 | async-start | bytes 1048576
  507.9 64.1 %copy-start.12 = (f32[64]{0:T(128)S(1)}, f32[64]{0:T(128)}, u32[]{:S(2)}) copy-start(f32[64]{0:T(128)} %param.25) | copy-start | bytes 772

commit v3 on v2

--- a/solution.py
+++ b/solution.py
@@ -11,6 +11,18 @@
     centered = values - average
     variance = jnp.mean(centered * centered, axis=reduce_axis, keepdims=True)
     return centered * lax.rsqrt(variance + 1e-05)
+
+
+def total_over(values, axis_name):
+    size = lax.axis_size(axis_name)
+    if size & (size - 1):
+        return lax.psum(values, axis_name)
+    step = 1
+    while step < size:
+        moves = [(d, d ^ step) for d in range(size)]
+        values = values + lax.ppermute(values, axis_name, moves)
+        step *= 2
+    return values
 
 
 def body(
@@ -73,22 +85,33 @@
 
     unit_chunk = left_proj.shape[1] // CHUNKS
     spans = [slice(t * unit_chunk, (t + 1) * unit_chunk) for t in range(CHUNKS)]
-    right_own = [in_half(factor(right_proj[:, t], right_gate[:, t]), 0, 1) for t in spans]
+    tie = lax.optimization_barrier
+    right_factor = tie(factor(right_proj, right_gate))
+    left_factor = factor(left_proj, left_gate)
+    right_own = []
+    right_other = []
+    for t in spans:
+        block = right_factor[t]
+        if right_own:
+            block, right_own[-1] = tie((block, right_own[-1]))
+        right_own.append(in_half(block, 0, 1))
+    left_factor, right_own[-1] = tie((left_factor, right_own[-1]))
     right_other = [lax.ppermute(block, "res", across) for block in right_own]
-    left_own = [in_half(factor(left_proj[:, t], left_gate[:, t]), 0, 1) for t in spans]
-    gating = lax.optimization_barrier(
-        jax.nn.sigmoid(
-            jnp.einsum("rkd,de->rke", normed, gate_weight, preferred_element_type=jnp.float32)
-        )
-    )
-
-    def updated_columns(right_blocks, start):
-        parts = []
-        for left_block, right_block in zip(left_own, right_blocks):
-            product = jnp.einsum(
+    left_own = [in_half(left_factor[t], 0, 1) for t in spans]
+    gating = jax.nn.sigmoid(
+        jnp.einsum("rkd,de->rke", normed, gate_weight, preferred_element_type=jnp.float32)
+    )
+
+    def products(right_blocks):
+        return [
+            jnp.einsum(
                 "cik,cjk->cij", left_block, right_block, preferred_element_type=jnp.float32
             ).astype(jnp.bfloat16)
-            parts.append(in_half(product, 1, 0))
+            for left_block, right_block in zip(left_own, right_blocks)
+        ]
+
+    def updated_columns(own_products, start):
+        parts = [in_half(product, 1, 0) for product in own_products]
         triangle_out = jnp.concatenate(parts, axis=0)
         normed_tri = (
             layer_norm(triangle_out.astype(jnp.float32), 0) * gain_out[:, None, None]
@@ -100,12 +123,16 @@
         pair_columns = lax.dynamic_slice_in_dim(crop_pair, start, half_columns, 1)
         return (pair_columns.astype(jnp.float32) + gate_columns * update).astype(jnp.bfloat16)
 
-    updated_own = updated_columns(right_own, own_start)
+    own_products, gating, mirror_targets, right_other[0] = tie(
+        (products(right_own), gating, mirror_targets, right_other[0])
+    )
+    updated_own = updated_columns(own_products, own_start)
+    updated_own, right_other[-1] = tie((updated_own, right_other[-1]))
     mirrored = jnp.zeros((crop_pair.shape[1], row_count, crop_pair.shape[2]), jnp.bfloat16)
     mirrored = lax.dynamic_update_slice_in_dim(
         mirrored, in_half(updated_own, 1, 0), own_start, 0
     )
-    updated_other = updated_columns(right_other, other_start)
+    updated_other = updated_columns(products(right_other), other_start)
     for shift in range(group):
         target = (place + shift) % group
         source = (place - shift) % group
@@ -145,9 +172,19 @@
     bias_part = jnp.sum(dlogits.astype(jnp.float32), axis=(1, 2))
     loss_part = jnp.sum(pair_mask * (log_total[0] - jnp.sum(target_hot * logits, axis=0)))
     count_part = jnp.sum(pair_mask)
-    head_total, bias_total, loss_total, count = lax.psum(
-        (head_part, bias_part, loss_part, count_part), ("res", "rep")
-    )
+    head_shape = head_part.shape
+    packed = jnp.concatenate(
+        [
+            head_part.reshape(-1, 128),
+            jnp.pad(bias_part, (0, 128 - bias_part.shape[0]))[None],
+            jnp.pad(jnp.stack([loss_part, count_part]), (0, 126))[None],
+        ],
+        axis=0,
+    )
+    packed = total_over(total_over(packed, "res"), "rep")
+    head_total = packed[:-2].reshape(head_shape)
+    bias_total = packed[-2, : bias_part.shape[0]]
+    loss_total, count = packed[-1, 0], packed[-1, 1]
     mean_loss = jnp.reshape(loss_total / count, (1,))
     return (updated[None], pair_grad[None], head_total / count, bias_total / count, mean_loss)
 

time: 636 us -> 613 us (0.964)
  matrix products: 117 us -> 78.2 us
  local copies, waits for them, and re-layouts: 53.4 us -> 81.8 us
  starting transfers between devices: 71.1 us -> 57.2 us
  blocking collectives: 39.9 us -> 33.2 us
    ppermute x2, waiting for transfers between devices: 153 us -> 90.6 us  [body(): right_other = [lax.ppermute(block, 'res', across) for block in right_own]]
    psum x1 -> x0, blocking collectives: 39.9 us -> none  [body(): lax.psum((head_part, bias_part, loss_part, count_part), ('res', 'rep'))]
    all_to_all x0 -> x1, blocking collectives: none -> 33.2 us  [in_half(): lax.all_to_all(values, 'res', split_axis=split_axis, concat_axis=concat_a...]
    slice x0 -> x6, local copies, waits for them, and re-layouts: none -> 33.1 us  [the longest x3 18.4 us: body(): left_own = [in_half(left_factor[t], 0, 1) for t in spans]]
    all_to_all x9 -> x8, waiting for transfers between devices: 98.2 us -> 128 us  [in_half(): lax.all_to_all(values, 'res', split_axis=split_axis, concat_axis=concat_a...]
    dot_general x4 -> x2, matrix products: 40.8 us -> 19.2 us  [factor(): jnp.einsum('rkd,dc->crk', normed, gating_weight, preferred_element_type=j...]
    ppermute x4, waiting for transfers between devices: 62.9 us -> 83.4 us  [body(): arrived = lax.ppermute(block, 'res', moves)]
    convert_element_type x9 -> x2, local copies, waits for them, and re-layouts: 22.3 us -> 4.1 us  [products(): return [jnp.einsum('cik,cjk->cij', left_block, right_block, preferred_ele...]
  transfers between devices with their start and end apart: 16 -> 20, of which waited for: 12 -> 15; matrix products, arithmetic and copies ran while one was open for 23% -> 20% of each run, Pallas kernels for 0% -> 0%
where the time goes in v3:
time: 613 us; the launch traced here: 604 us
  waiting for transfers between devices  316 us (52%)
  local copies, waits for them, and re-layouts  81.8 us (13%)
  matrix products  78.2 us (13%)
  starting transfers between devices  57.2 us (9%)
  other arithmetic  33.6 us (5%)
  blocking collectives  33.2 us (5%)
    all_to_all x8, waiting for transfers between devices, in_half(): lax.all_to_all(values, 'res', split_axis=split_axis, concat_axis=concat_a...  128 us
    ppermute x2, waiting for transfers between devices, body(): right_other = [lax.ppermute(block, 'res', across) for block in right_own]  90.6 us
    ppermute x4, waiting for transfers between devices, body(): arrived = lax.ppermute(block, 'res', moves)  83.4 us
    all_to_all x8, starting transfers between devices, in_half(): lax.all_to_all(values, 'res', split_axis=split_axis, concat_axis=concat_a...  35.4 us
    all_to_all x1, blocking collectives, in_half(): lax.all_to_all(values, 'res', split_axis=split_axis, concat_axis=concat_a...  33.2 us
    dot_general x2, matrix products, factor(): jnp.einsum('rkd,dc->crk', normed, project_weight, preferred_element_type=...  21.1 us
    dot_general x2, matrix products, factor(): jnp.einsum('rkd,dc->crk', normed, gating_weight, preferred_element_type=j...  19.2 us
    slice x3, local copies, waits for them, and re-layouts, body(): left_own = [in_half(left_factor[t], 0, 1) for t in spans]  18.4 us
  transfers between devices with their start and end apart: 20, of which 15 were waited for; matrix products, arithmetic and copies ran while one was open for 20% of the time, Pallas kernels for 0%

profile of v3, /device:TPU:0, one launch (start us, length us, event | category | flops | bytes accessed | tf_op | source)
XLA Modules:
  0.0 604.2 jit_solution(1165117710330025191)
XLA Ops:
  2.1 3.8 convert_reduce_fusion
  5.9 5.5 fusion.3
  11.6 9.5 %fusion.52 = f32[48,384,128]{2,1,0:T(8,128)S(1)} fusion(bf16[128,128]{1,0:T(8,128)(2,1)S(1)} %copy-done.14, bf16[1,48,384,128]{3,2,1,0:T(8,128)(2,1)} %param.13, f32[128]{0:T(128)S(1)} %copy-done.17, f32[48,384]{1,0:T(8,128)S(1)} %get-tuple-element.69, f32[48,384]{1,0:T(8,128)S(1)} %broadcast_multiply_fusion.1), kind=kOutput, calls=%fused_computation.85 | convolution fusion | flops 615776256 | bytes 14336512 | tf_op jit(solution)/shard_map/rkd,dc->crk/dot_general | solution.py:72
  21.1 10.6 %fusion.28 = bf16[128,48,384]{0,2,1:T(8,128)(2,1)} fusion(f32[48,384]{1,0:T(8,128)S(1)} %get-tuple-element.70, f32[48,384,128]{2,1,0:T(8,128)S(1)} %fusion.52, bf16[128,128]{1,0:T(8,128)(2,1)S(1)} %copy-done.22, bf16[1,48,384,128]{3,2,1,0:T(8,128)(2,1)S(1)} %bitcast.160, f32[128]{0:T(128)S(1)} %copy-done.17, f32[48,384]{1,0:T(8,128)S(1)} %get-tuple-element.69, ...), kind=kOutput, calls=%fused_computation.50 | convolution fusion | flops 629932032 | bytes 19128832 | tf_op jit(solution)/shard_map/rkd,dc->crk/dot_general | solution.py:68
  31.7 9.1 %fusion.70 = (bf16[64,48,384]{0,2,1:T(8,128)(2,1)}, bf16[64,48,384]{0,2,1:T(8,128)(2,1)}) fusion(bf16[128,48,384]{0,2,1:T(8,128)(2,1)} %fusion.28), kind=kLoop, calls=%fused_computation.113 | loop fusion | bytes 9437184 | tf_op jit(solution)/shard_map/slice | solution.py:94
  40.8 5.0 copy.109
  45.8 33.2 %all_to_all.181 = bf16[64,48,384]{2,1,0:T(8,128)(2,1)S(1)} all-to-all(bf16[64,48,384]{2,1,0:T(8,128)(2,1)S(1)} %copy.109), channel_id=1, replica_groups={{0,4,8,12},{16,20,24,28},{1,5,9,13},{17,21,25,29},{2,6,10,14},{18,22,26..., dimensions={0} | all-to-all | bytes 4718592 | tf_op jit(solution)/shard_map/all_to_all | solution.py:77
  80.8 6.2 %copy.111 = bf16[64,48,384]{2,1,0:T(8,128)(2,1)} copy(bf16[64,48,384]{0,2,1:T(8,128)(2,1)} %get-tuple-element.16) | data formatting | bytes 4718592 | tf_op jit(solution)/shard_map/optimization_barrier | solution.py:96
  87.0 3.8 all-to-all-start.1
  91.8 9.7 %fusion.55 = f32[48,384,128]{2,1,0:T(8,128)S(1)} fusion(bf16[128,128]{1,0:T(8,128)(2,1)} %param.18, bf16[1,48,384,128]{3,2,1,0:T(8,128)(2,1)} %param.13, f32[128]{0:T(128)S(1)} %copy-done.17, f32[48,384]{1,0:T(8,128)S(1)} %get-tuple-element.69, f32[48,384]{1,0:T(8,128)S(1)} %broadcast_multiply_fusion.1), kind=kOutput, calls=%fused_computation.88 | convolution fusion | flops 615776256 | bytes 14336512 | tf_op jit(solution)/shard_map/rkd,dc->crk/dot_general | solution.py:72
  101.6 10.6 %fusion.27 = bf16[128,48,384]{0,2,1:T(8,128)(2,1)} fusion(f32[48,384]{1,0:T(8,128)S(1)} %copy-done.12, f32[48,384,128]{2,1,0:T(8,128)S(1)} %fusion.55, bf16[128,128]{1,0:T(8,128)(2,1)S(1)} %copy-done.23, bf16[1,48,384,128]{3,2,1,0:T(8,128)(2,1)S(1)} %bitcast.162, f32[128]{0:T(128)S(1)} %copy-done.17, f32[48,384]{1,0:T(8,128)S(1)} %get-tuple-element.69, ...), kind=kOutput, calls=%fused_computation.49 | convolution fusion | flops 629932032 | bytes 19128832 | tf_op jit(solution)/shard_map/rkd,dc->crk/dot_general | solution.py:68
  112.1 5.0 all-to-all-done.1
  117.2 4.8 all-to-all-start.4
  125.1 5.9 fusion.69
  131.0 6.3 %copy.115 = bf16[64,48,384]{2,1,0:T(8,128)(2,1)} copy(bf16[64,48,384]{0,2,1:T(8,128)(2,1)} %get-tuple-element.55) | data formatting | bytes 4718592 | tf_op jit(solution)/shard_map/slice | solution.py:100
  137.3 4.2 all-to-all-start.3
  141.5 6.3 %copy.113 = bf16[64,48,384]{2,1,0:T(8,128)(2,1)} copy(bf16[64,48,384]{0,2,1:T(8,128)(2,1)} %get-tuple-element.56) | data formatting | bytes 4718592 | tf_op jit(solution)/shard_map/slice | solution.py:100
  147.8 21.0 %all-to-all-done.3 = bf16[64,48,384]{2,1,0:T(8,128)(2,1)S(1)} async-done(((bf16[64,48,384]{2,1,0:T(8,128)(2,1)}), bf16[64,48,384]{2,1,0:T(8,128)(2,1)S(1)}, u32[]{:S(2)}, u32[]{:S(2)}) %all-to-all-start.3) | async-done | bytes 2359328 | tf_op jit(solution)/shard_map/all_to_all | solution.py:77
  168.8 5.0 all-to-all-start.2
  176.4 10.9 %add_divide_fusion = f32[48,384,128]{2,1,0:T(8,128)} fusion(bf16[128,128]{1,0:T(8,128)(2,1)S(1)} %copy-done.24, bf16[1,48,384,128]{3,2,1,0:T(8,128)(2,1)} %param.13, f32[128]{0:T(128)S(1)} %copy-done.17, f32[48,384]{1,0:T(8,128)S(1)} %get-tuple-element.69, f32[48,384]{1,0:T(8,128)S(1)} %broadcast_multiply_fusion.1), kind=kOutput, calls=%fused_computation.12 | convolution fusion | flops 622854144 | bytes 14336512 | tf_op jit(solution)/shard_map/rkd,de->rke/dot_general | solution.py:102
  191.0 37.7 %all-to-all-done.2 = bf16[64,48,384]{2,1,0:T(8,128)(2,1)} async-done(((bf16[64,48,384]{2,1,0:T(8,128)(2,1)}), bf16[64,48,384]{2,1,0:T(8,128)(2,1)}, u32[]{:S(2)}, u32[]{:S(2)}) %all-to-all-start.2) | async-done | bytes 2359328 | tf_op jit(solution)/shard_map/all_to_all | solution.py:77
  230.8 3.5 convolution_convert_fusion.3
  236.6 41.2 %collective-permute-done = bf16[16,192,384]{2,1,0:T(8,128)(2,1)} collective-permute-done((bf16[16,192,384]{2,1,0:T(8,128)(2,1)}, bf16[16,192,384]{2,1,0:T(8,128)(2,1)}, u32[]{:S(2)}, u32[]{:S(2)}) %collective-permute-start) | collective-permute-done | bytes 2359328 | tf_op jit(solution)/shard_map/ppermute | solution.py:99
  279.8 4.5 all-to-all-start.5
  284.3 3.4 copy.122
  287.8 14.8 %all-to-all-done.5 = bf16[16,192,192]{2,0,1:T(8,128)(2,1)} async-done(((bf16[16,192,192]{2,0,1:T(8,128)(2,1)}), bf16[16,192,192]{2,0,1:T(8,128)(2,1)}, u32[]{:S(2)}, u32[]{:S(2)}) %all-to-all-start.5) | async-done | bytes 1179680 | tf_op jit(solution)/shard_map/all_to_all | solution.py:77
  302.5 4.3 all-to-all-start.6
  306.9 3.4 collective-permute-start.1
  317.0 27.2 %all-to-all-done.6 = bf16[16,192,192]{2,0,1:T(8,128)(2,1)} async-done(((bf16[16,192,192]{2,0,1:T(8,128)(2,1)}), bf16[16,192,192]{2,0,1:T(8,128)(2,1)}, u32[]{:S(2)}, u32[]{:S(2)}) %all-to-all-start.6) | async-done | bytes 1179680 | tf_op jit(solution)/shard_map/all_to_all | solution.py:77
  344.2 4.5 all-to-all-start.7
  352.5 4.2 fusion.16
  356.8 4.4 fusion.22
  361.2 49.4 %collective-permute-done.1 = bf16[16,192,384]{2,1,0:T(8,128)(2,1)} collective-permute-done((bf16[16,192,384]{2,1,0:T(8,128)(2,1)}, bf16[16,192,384]{2,1,0:T(8,128)(2,1)}, u32[]{:S(2)}, u32[]{:S(2)}) %collective-permute-start.1) | collective-permute-done | bytes 2359328 | tf_op jit(solution)/shard_map/ppermute | solution.py:99
  410.6 2.7 convolution_convert_fusion
  415.3 4.4 all-to-all-start.8
  419.7 2.9 copy.133
  422.6 14.2 %all-to-all-done.8 = bf16[16,192,192]{2,0,1:T(8,128)(2,1)} async-done(((bf16[16,192,192]{2,0,1:T(8,128)(2,1)}), bf16[16,192,192]{2,0,1:T(8,128)(2,1)}, u32[]{:S(2)}, u32[]{:S(2)}) %all-to-all-start.8) | async-done | bytes 1179680 | tf_op jit(solution)/shard_map/all_to_all | solution.py:77
  436.8 4.7 all-to-all-start.9
  449.1 4.2 fusion.13
  464.0 3.4 collective-permute-start.4
  469.0 7.8 %all-to-all-done.9 = bf16[48,192,128]{2,0,1:T(8,128)(2,1)} async-done(((bf16[48,192,128]{2,0,1:T(8,128)(2,1)}), bf16[48,192,128]{2,0,1:T(8,128)(2,1)}, u32[]{:S(2)}, u32[]{:S(2)}) %all-to-all-start.9) | async-done | bytes 2359328 | tf_op jit(solution)/shard_map/all_to_all | solution.py:77
  480.6 47.0 %collective-permute-done.2 = bf16[48,48,128]{2,1,0:T(8,128)(2,1)S(1)} collective-permute-done((bf16[48,48,128]{2,1,0:T(8,128)(2,1)}, bf16[48,48,128]{2,1,0:T(8,128)(2,1)S(1)}, u32[]{:S(2)}, u32[]{:S(2)}) %collective-permute-start.2) | collective-permute-done | bytes 589856 | tf_op jit(solution)/shard_map/ppermute | solution.py:144
  528.2 36.5 %collective-permute-done.5 = bf16[48,48,128]{2,1,0:T(8,128)(2,1)S(1)} collective-permute-done((bf16[48,48,128]{2,1,0:T(8,128)(2,1)S(1)}, bf16[48,48,128]{2,1,0:T(8,128)(2,1)S(1)}, u32[]{:S(2)}, u32[]{:S(2)}) %collective-permute-start.5) | collective-permute-done | bytes 589856 | tf_op jit(solution)/shard_map/ppermute | solution.py:144
  569.9 4.0 convert_reduce_fusion.3
  576.9 3.9 collective-permute-done.6
  581.0 4.1 collective-permute-done.7
  585.1 4.8 collective-permute-done.8
  592.7 5.3 convert_bitcast_fusion.1
  (160 shorter events, 70.9 us)
Async XLA Ops:
  0.6 356.1 %copy-start = (bf16[128,128]{1,0:T(8,128)(2,1)S(1)}, bf16[128,128]{1,0:T(8,128)(2,1)}, u32[]{:S(2)}) copy-start(bf16[128,128]{1,0:T(8,128)(2,1)} %param.23) | copy-start | bytes 98308
  2.0 9.5 %copy-start.15 = (f32[384]{0:T(512)}, f32[384]{0:T(512)S(1)}, u32[]{:S(2)}) copy-start(f32[384]{0:T(512)S(1)} %convert_reduce_fusion.4) | copy-start | bytes 4612
  2.1 9.5 %copy-start.14 = (bf16[128,128]{1,0:T(8,128)(2,1)S(1)}, bf16[128,128]{1,0:T(8,128)(2,1)}, u32[]{:S(2)}) copy-start(bf16[128,128]{1,0:T(8,128)(2,1)} %param.20) | copy-start | bytes 98308
  2.1 9.5 %copy-start.17 = (f32[128]{0:T(128)S(1)}, f32[128]{0:T(128)}, u32[]{:S(2)}) copy-start(f32[128]{0:T(128)} %param.16) | copy-start | bytes 1540
  5.9 15.2 %slice-start = ((s8[4718592]{0:T(1024)(128)(4,1)}), s8[524288]{0:T(1024)(128)(4,1)S(1)}, s32[]{:S(2)}) async-start(s8[4718592]{0:T(1024)(128)(4,1)} %bitcast.159), calls=%async_computation.10 | async-start | bytes 1048576
  11.5 9.6 %copy-start.20 = (f32[48]{0:T(128)}, f32[48]{0:T(128)S(1)}, u32[]{:S(2)}) copy-start(f32[48]{0:T(128)S(1)} %fusion.59) | copy-start | bytes 580
  11.6 9.5 %copy-start.11 = (f32[48,384]{1,0:T(8,128)}, f32[48,384]{1,0:T(8,128)S(1)}, u32[]{:S(2)}) copy-start(f32[48,384]{1,0:T(8,128)S(1)} %get-tuple-element.70) | copy-start | bytes 221188
  11.6 9.5 %slice-start.1 = ((s8[4718592]{0:T(1024)(128)(4,1)}), s8[4194304]{0:T(1024)(128)(4,1)S(1)}, s32[]{:S(2)}) async-start(s8[4718592]{0:T(1024)(128)(4,1)} %bitcast.159), calls=%async_computation.11 | async-start | bytes 8388608
  11.6 9.5 %copy-start.22 = (bf16[128,128]{1,0:T(8,128)(2,1)S(1)}, bf16[128,128]{1,0:T(8,128)(2,1)}, u32[]{:S(2)}) copy-start(bf16[128,128]{1,0:T(8,128)(2,1)} %param.19) | copy-start | bytes 98308
  80.8 10.0 %copy-start.10 = (s32[1,48,384]{2,1,0:T(8,128)S(1)}, s32[1,48,384]{2,1,0:T(8,128)}, u32[]{:S(2)}) copy-start(s32[1,48,384]{2,1,0:T(8,128)} %param.15) | copy-start | bytes 221188
  87.0 14.5 %slice-start.2 = ((s8[4718592]{0:T(1024)(128)(4,1)}), s8[524288]{0:T(1024)(128)(4,1)S(1)}, s32[]{:S(2)}) async-start(s8[4718592]{0:T(1024)(128)(4,1)} %bitcast.161), calls=%async_computation.12 | async-start | bytes 1048576
  87.0 30.2 %all-to-all-start.1 = ((bf16[64,48,384]{2,1,0:T(8,128)(2,1)}), bf16[64,48,384]{2,1,0:T(8,128)(2,1)S(1)}, u32[]{:S(2)}, u32[]{:S(2)}) async-start(bf16[64,48,384]{2,1,0:T(8,128)(2,1)} %copy.111), calls=%async_computation.1 | async-start | bytes 4718592 | tf_op jit(solution)/shard_map/all_to_all | solution.py:77
  91.8 9.7 %slice-start.3 = ((s8[4718592]{0:T(1024)(128)(4,1)}), s8[4194304]{0:T(1024)(128)(4,1)S(1)}, s32[]{:S(2)}) async-start(s8[4718592]{0:T(1024)(128)(4,1)} %bitcast.161), calls=%async_computation.13 | async-start | bytes 8388608
  91.8 9.7 %copy-start.12 = (f32[48,384]{1,0:T(8,128)S(1)}, f32[48,384]{1,0:T(8,128)}, u32[]{:S(2)}) copy-start(f32[48,384]{1,0:T(8,128)} %copy-done.11) | copy-start | bytes 221188
  91.8 9.7 %copy-start.23 = (bf16[128,128]{1,0:T(8,128)(2,1)S(1)}, bf16[128,128]{1,0:T(8,128)(2,1)}, u32[]{:S(2)}) copy-start(bf16[128,128]{1,0:T(8,128)(2,1)} %param.17) | copy-start | bytes 98308
  117.2 20.1 %all-to-all-start.4 = ((s32[8,1,2304]{2,1,0:T(1,128)}), s32[8,1,2304]{2,1,0:T(1,128)S(1)}, u32[]{:S(2)}, u32[]{:S(2)}) async-start(s32[8,1,2304]{2,1,0:T(1,128)} %reshape.125), calls=%async_computation.4 | async-start | bytes 147456 | tf_op jit(solution)/shard_map/all_to_all | solution.py:53
  137.3 31.4 %all-to-all-start.3 = ((bf16[64,48,384]{2,1,0:T(8,128)(2,1)}), bf16[64,48,384]{2,1,0:T(8,128)(2,1)S(1)}, u32[]{:S(2)}, u32[]{:S(2)}) async-start(bf16[64,48,384]{2,1,0:T(8,128)(2,1)} %copy.115), calls=%async_computation.3 | async-start | bytes 4718592 | tf_op jit(solution)/shard_map/all_to_all | solution.py:77
  141.5 34.9 %copy-start.24 = (bf16[128,128]{1,0:T(8,128)(2,1)S(1)}, bf16[128,128]{1,0:T(8,128)(2,1)}, u32[]{:S(2)}) copy-start(bf16[128,128]{1,0:T(8,128)(2,1)} %param.21) | copy-start | bytes 98308
  168.7 18.6 %copy-start.9 = (bf16[64,48,384]{2,1,0:T(8,128)(2,1)}, bf16[64,48,384]{2,1,0:T(8,128)(2,1)S(1)}, u32[]{:S(2)}) copy-start(bf16[64,48,384]{2,1,0:T(8,128)(2,1)S(1)} %all-to-all-done.3) | copy-start | bytes 7077892
  168.8 59.9 %all-to-all-start.2 = ((bf16[64,48,384]{2,1,0:T(8,128)(2,1)}), bf16[64,48,384]{2,1,0:T(8,128)(2,1)}, u32[]{:S(2)}, u32[]{:S(2)}) async-start(bf16[64,48,384]{2,1,0:T(8,128)(2,1)} %copy.113), calls=%async_computation.2 | async-start | bytes 4718592 | tf_op jit(solution)/shard_map/all_to_all | solution.py:77
  173.7 104.0 %collective-permute-start = (bf16[16,192,384]{2,1,0:T(8,128)(2,1)}, bf16[16,192,384]{2,1,0:T(8,128)(2,1)}, u32[]{:S(2)}, u32[]{:S(2)}) collective-permute-start(bf16[16,192,384]{2,1,0:T(8,128)(2,1)} %bitcast.11), channel_id=1, source_target_pairs={{0,16},{4,20},{8,24},{12,28},{16,0},{20,4},{24,8},{28,12},{1,17},{... | collective-permute-start | bytes 7077896 | tf_op jit(solution)/shard_map/ppermute | solution.py:99
  191.0 43.4 %copy-start.3 = (bf16[16,4,48,384]{3,2,1,0:T(8,128)(2,1)}, bf16[16,4,48,384]{3,2,1,0:T(8,128)(2,1)S(1)}, u32[]{:S(2)}) copy-start(bf16[16,4,48,384]{3,2,1,0:T(8,128)(2,1)S(1)} %copy.116) | copy-start | bytes 7077892
  228.6 5.7 copy-start.8
  279.8 30.5 %copy-start.6 = (bf16[16,4,48,384]{3,2,1,0:T(8,128)(2,1)S(1)}, bf16[16,4,48,384]{3,2,1,0:T(8,128)(2,1)}, u32[]{:S(2)}) copy-start(bf16[16,4,48,384]{3,2,1,0:T(8,128)(2,1)} %copy-done.5) | copy-start | bytes 7077892
  279.8 22.7 %all-to-all-start.5 = ((bf16[16,192,192]{2,0,1:T(8,128)(2,1)}), bf16[16,192,192]{2,0,1:T(8,128)(2,1)}, u32[]{:S(2)}, u32[]{:S(2)}) async-start(bf16[16,192,192]{2,0,1:T(8,128)(2,1)} %copy.119), calls=%async_computation.5 | async-start | bytes 3145728 | tf_op jit(solution)/shard_map/all_to_all | solution.py:77
  302.5 41.7 %all-to-all-start.6 = ((bf16[16,192,192]{2,0,1:T(8,128)(2,1)}), bf16[16,192,192]{2,0,1:T(8,128)(2,1)}, u32[]{:S(2)}, u32[]{:S(2)}) async-start(bf16[16,192,192]{2,0,1:T(8,128)(2,1)} %copy.122), calls=%async_computation.6 | async-start | bytes 3145728 | tf_op jit(solution)/shard_map/all_to_all | solution.py:77
  306.9 103.7 %collective-permute-start.1 = (bf16[16,192,384]{2,1,0:T(8,128)(2,1)}, bf16[16,192,384]{2,1,0:T(8,128)(2,1)}, u32[]{:S(2)}, u32[]{:S(2)}) collective-permute-start(bf16[16,192,384]{2,1,0:T(8,128)(2,1)} %bitcast.186), channel_id=1, source_target_pairs={{0,16},{4,20},{8,24},{12,28},{16,0},{20,4},{24,8},{28,12},{1,17},{... | collective-permute-start | bytes 7077896 | tf_op jit(solution)/shard_map/ppermute | solution.py:99
  344.2 71.1 %all-to-all-start.7 = ((bf16[16,192,192]{2,0,1:T(8,128)(2,1)}), bf16[16,192,192]{2,0,1:T(8,128)(2,1)}, u32[]{:S(2)}, u32[]{:S(2)}) async-start(bf16[16,192,192]{2,0,1:T(8,128)(2,1)} %copy.126), calls=%async_computation.7 | async-start | bytes 3145728 | tf_op jit(solution)/shard_map/all_to_all | solution.py:77
  350.7 6.0 slice-start.4
  356.8 53.8 %copy-start.4 = (bf16[16,4,48,384]{3,2,1,0:T(8,128)(2,1)S(1)}, bf16[16,4,48,384]{3,2,1,0:T(8,128)(2,1)}, u32[]{:S(2)}) copy-start(bf16[16,4,48,384]{3,2,1,0:T(8,128)(2,1)} %copy-done.3) | copy-start | bytes 7077892
  415.3 21.5 %all-to-all-start.8 = ((bf16[16,192,192]{2,0,1:T(8,128)(2,1)}), bf16[16,192,192]{2,0,1:T(8,128)(2,1)}, u32[]{:S(2)}, u32[]{:S(2)}) async-start(bf16[16,192,192]{2,0,1:T(8,128)(2,1)} %copy.129), calls=%async_computation.8 | async-start | bytes 3145728 | tf_op jit(solution)/shard_map/all_to_all | solution.py:77
  436.8 40.0 %all-to-all-start.9 = ((bf16[48,192,128]{2,0,1:T(8,128)(2,1)}), bf16[48,192,128]{2,0,1:T(8,128)(2,1)}, u32[]{:S(2)}, u32[]{:S(2)}) async-start(bf16[48,192,128]{2,0,1:T(8,128)(2,1)} %copy.133), calls=%async_computation.9 | async-start | bytes 4718592 | tf_op jit(solution)/shard_map/all_to_all | solution.py:77
  443.6 9.8 %slice-start.10 = ((s8[9437184]{0:T(1024)(128)(4,1)}), s8[4194304]{0:T(1024)(128)(4,1)S(1)}, s32[]{:S(2)}) async-start(s8[9437184]{0:T(1024)(128)(4,1)} %bitcast.192), calls=%async_computation.20 | async-start | bytes 8388608
  444.7 8.7 %slice-start.11 = ((s8[9437184]{0:T(1024)(128)(4,1)}), s8[4194304]{0:T(1024)(128)(4,1)S(1)}, s32[]{:S(2)}) async-start(s8[9437184]{0:T(1024)(128)(4,1)} %bitcast.192), calls=%async_computation.21 | async-start | bytes 8388608
  447.3 6.1 %slice-start.6 = ((s8[4718592]{0:T(1024)(128)(4,1)}), s8[4194304]{0:T(1024)(128)(4,1)S(1)}, s32[]{:S(2)}) async-start(s8[4718592]{0:T(1024)(128)(4,1)} %bitcast.165), calls=%async_computation.16 | async-start | bytes 8388608
  459.7 67.9 %collective-permute-start.2 = (bf16[48,48,128]{2,1,0:T(8,128)(2,1)}, bf16[48,48,128]{2,1,0:T(8,128)(2,1)S(1)}, u32[]{:S(2)}, u32[]{:S(2)}) collective-permute-start(bf16[48,48,128]{2,1,0:T(8,128)(2,1)} %get-tuple-element.62), channel_id=1, source_target_pairs={{0,16},{4,20},{8,24},{12,28},{16,0},{20,4},{24,8},{28,12},{1,17},{... | collective-permute-start | bytes 1769480 | tf_op jit(solution)/shard_map/ppermute | solution.py:144
  462.2 65.6 %collective-permute-start.3 = (bf16[48,48,128]{2,1,0:T(8,128)(2,1)}, bf16[48,48,128]{2,1,0:T(8,128)(2,1)S(1)}, u32[]{:S(2)}, u32[]{:S(2)}) collective-permute-start(bf16[48,48,128]{2,1,0:T(8,128)(2,1)} %get-tuple-element.61), channel_id=1, source_target_pairs={{0,20},{4,24},{8,28},{12,16},{16,4},{20,8},{24,12},{28,0},{1,21},{... | collective-permute-start | bytes 1769480 | tf_op jit(solution)/shard_map/ppermute | solution.py:144
  464.0 64.0 %collective-permute-start.4 = (bf16[48,48,128]{2,1,0:T(8,128)(2,1)}, bf16[48,48,128]{2,1,0:T(8,128)(2,1)S(1)}, u32[]{:S(2)}, u32[]{:S(2)}) collective-permute-start(bf16[48,48,128]{2,1,0:T(8,128)(2,1)} %get-tuple-element.60), channel_id=1, source_target_pairs={{0,24},{4,28},{8,16},{12,20},{16,8},{20,12},{24,0},{28,4},{1,25},{... | collective-permute-start | bytes 1769480 | tf_op jit(solution)/shard_map/ppermute | solution.py:144
  467.4 97.2 %collective-permute-start.5 = (bf16[48,48,128]{2,1,0:T(8,128)(2,1)S(1)}, bf16[48,48,128]{2,1,0:T(8,128)(2,1)S(1)}, u32[]{:S(2)}, u32[]{:S(2)}) collective-permute-start(bf16[48,48,128]{2,1,0:T(8,128)(2,1)S(1)} %get-tuple-element.59), channel_id=1, source_target_pairs={{0,28},{4,16},{8,20},{12,24},{16,12},{20,0},{24,4},{28,8},{1,29},{... | collective-permute-start | bytes 1769480 | tf_op jit(solution)/shard_map/ppermute | solution.py:144
  479.1 85.7 %slice-start.8 = ((s8[4718592]{0:T(1024)(128)(4,1)}), s8[4194304]{0:T(1024)(128)(4,1)S(1)}, s32[]{:S(2)}) async-start(s8[4718592]{0:T(1024)(128)(4,1)} %bitcast.168), calls=%async_computation.18 | async-start | bytes 8388608
  480.3 84.6 %slice-start.9 = ((s8[4718592]{0:T(1024)(128)(4,1)}), s8[524288]{0:T(1024)(128)(4,1)S(1)}, s32[]{:S(2)}) async-start(s8[4718592]{0:T(1024)(128)(4,1)} %bitcast.168), calls=%async_computation.19 | async-start | bytes 1048576
  480.3 84.6 %copy-start.13 = (bf16[128,64]{0,1:T(8,128)(2,1)S(1)}, bf16[128,64]{0,1:T(8,128)(2,1)}, u32[]{:S(2)}) copy-start(bf16[128,64]{0,1:T(8,128)(2,1)} %param.24) | copy-start | bytes 49156
  480.3 84.6 %copy-start.18 = (f32[64]{0:T(128)S(1)}, f32[64]{0:T(128)}, u32[]{:S(2)}) copy-start(f32[64]{0:T(128)} %param.25) | copy-start | bytes 772
  576.9 4.0 collective-permute-start.6
  580.9 4.2 collective-permute-start.7
  585.1 4.9 collective-permute-start.8
  590.0 1.2 collective-permute-start.9
  591.2 6.9 %collective-permute-start.10 = (f32[66,128]{1,0:T(8,128)S(1)}, f32[66,128]{1,0:T(8,128)S(1)}, u32[]{:S(2)}, u32[]{:S(2)}) collective-permute-start(f32[66,128]{1,0:T(8,128)S(1)} %add.218), channel_id=1, source_target_pairs={{0,2},{1,3},{2,0},{3,1},{4,6},{5,7},{6,4},{7,5},{8,10},{9,11},{10,... | collective-permute-start | bytes 101384 | tf_op jit(solution)/shard_map/ppermute | solution.py:23
  (10 other events, 39.4 us)

commit v4 on v3

--- a/solution.py
+++ b/solution.py
@@ -83,36 +83,23 @@
             tiled=True,
         )
 
-    unit_chunk = left_proj.shape[1] // CHUNKS
+    tie = lax.optimization_barrier
+    right_own = in_half(factor(right_proj, right_gate), 0, 1)
+    left_factor, right_own = tie((factor(left_proj, left_gate), right_own))
+    unit_chunk = right_own.shape[0] // CHUNKS
     spans = [slice(t * unit_chunk, (t + 1) * unit_chunk) for t in range(CHUNKS)]
-    tie = lax.optimization_barrier
-    right_factor = tie(factor(right_proj, right_gate))
-    left_factor = factor(left_proj, left_gate)
-    right_own = []
-    right_other = []
-    for t in spans:
-        block = right_factor[t]
-        if right_own:
-            block, right_own[-1] = tie((block, right_own[-1]))
-        right_own.append(in_half(block, 0, 1))
-    left_factor, right_own[-1] = tie((left_factor, right_own[-1]))
-    right_other = [lax.ppermute(block, "res", across) for block in right_own]
-    left_own = [in_half(left_factor[t], 0, 1) for t in spans]
+    right_other = [lax.ppermute(right_own[t], "res", across) for t in spans]
+    left_own = in_half(left_factor, 0, 1)
     gating = jax.nn.sigmoid(
         jnp.einsum("rkd,de->rke", normed, gate_weight, preferred_element_type=jnp.float32)
     )
 
-    def products(right_blocks):
-        return [
-            jnp.einsum(
-                "cik,cjk->cij", left_block, right_block, preferred_element_type=jnp.float32
-            ).astype(jnp.bfloat16)
-            for left_block, right_block in zip(left_own, right_blocks)
-        ]
-
-    def updated_columns(own_products, start):
-        parts = [in_half(product, 1, 0) for product in own_products]
-        triangle_out = jnp.concatenate(parts, axis=0)
+    def product(left_block, right_block):
+        return jnp.einsum(
+            "cik,cjk->cij", left_block, right_block, preferred_element_type=jnp.float32
+        ).astype(jnp.bfloat16)
+
+    def updated_columns(triangle_out, start):
         normed_tri = (
             layer_norm(triangle_out.astype(jnp.float32), 0) * gain_out[:, None, None]
         ).astype(jnp.bfloat16)
@@ -123,16 +110,26 @@
         pair_columns = lax.dynamic_slice_in_dim(crop_pair, start, half_columns, 1)
         return (pair_columns.astype(jnp.float32) + gate_columns * update).astype(jnp.bfloat16)
 
-    own_products, gating, mirror_targets, right_other[0] = tie(
-        (products(right_own), gating, mirror_targets, right_other[0])
-    )
-    updated_own = updated_columns(own_products, own_start)
-    updated_own, right_other[-1] = tie((updated_own, right_other[-1]))
+    own_product, gating, mirror_targets, right_other[0] = tie(
+        (product(left_own, right_own), gating, mirror_targets, right_other[0])
+    )
+    own_part = in_half(own_product, 1, 0)
+    first_part = in_half(product(left_own[spans[0]], right_other[0]), 1, 0)
+    own_part, first_part, right_other[1] = tie((own_part, first_part, right_other[1]))
+    updated_own = updated_columns(own_part, own_start)
+    second_part = in_half(product(left_own[spans[1]], right_other[1]), 1, 0)
+    other_part = jnp.concatenate(
+        [
+            part.reshape((group, unit_chunk) + part.shape[1:])
+            for part in (first_part, second_part)
+        ],
+        axis=1,
+    ).reshape(own_part.shape)
     mirrored = jnp.zeros((crop_pair.shape[1], row_count, crop_pair.shape[2]), jnp.bfloat16)
     mirrored = lax.dynamic_update_slice_in_dim(
         mirrored, in_half(updated_own, 1, 0), own_start, 0
     )
-    updated_other = updated_columns(products(right_other), other_start)
+    updated_other = updated_columns(other_part, other_start)
     for shift in range(group):
         target = (place + shift) % group
         source = (place - shift) % group

time: 613 us -> 590 us (0.962)
  waiting for transfers between devices: 316 us -> 351 us
  blocking collectives: 33.2 us -> 0 us
  local copies, waits for them, and re-layouts: 81.8 us -> 70 us
  starting transfers between devices: 57.2 us -> 48.6 us
    all_to_all x8 -> x6, waiting for transfers between devices: 128 us -> 244 us  [in_half(): lax.all_to_all(values, 'res', split_axis=split_axis, concat_axis=concat_a...]
    ppermute x2, waiting for transfers between devices: 90.6 us -> 28.8 us  [body(): right_other = [lax.ppermute(right_own[t], 'res', across) for t in spans]]
    all_to_all x1 -> x0, blocking collectives: 33.2 us -> none  [in_half(): lax.all_to_all(values, 'res', split_axis=split_axis, concat_axis=concat_a...]
    ppermute x4, waiting for transfers between devices: 83.4 us -> 63.8 us  [body(): arrived = lax.ppermute(block, 'res', moves)]
    slice x5 -> x4, local copies, waits for them, and re-layouts: 32.5 us -> 13.4 us  [the longest x2 7.79 us: body(): second_part = in_half(product(left_own[spans[1]], right_other[1]), 1, 0)]
    convert_element_type x2 -> x4, local copies, waits for them, and re-layouts: 4.1 us -> 14 us  [the longest x1 6.96 us: factor(): return (gated * projected * pair_mask[None]).astype(jnp.bfloat16)]
    all_to_all x8 -> x6, starting transfers between devices: 35.4 us -> 27.9 us  [in_half(): lax.all_to_all(values, 'res', split_axis=split_axis, concat_axis=concat_a...]
    optimization_barrier x4 -> x2, local copies, waits for them, and re-layouts: 14.6 us -> 10.4 us  [the longest x1 6.96 us: body(): left_factor, right_own = tie((factor(left_proj, left_gate), right_own))]
  transfers between devices with their start and end apart: 20 -> 18, of which waited for: 15 -> 15; matrix products, arithmetic and copies ran while one was open for 20% -> 16% of each run, Pallas kernels for 0% -> 0%
where the time goes in v4:
time: 590 us; the launch traced here: 583 us
  waiting for transfers between devices  351 us (59%)
  matrix products  77.8 us (13%)
  local copies, waits for them, and re-layouts  70 us (12%)
  starting transfers between devices  48.6 us (8%)
  other arithmetic  31 us (5%)
    all_to_all x6, waiting for transfers between devices, in_half(): lax.all_to_all(values, 'res', split_axis=split_axis, concat_axis=concat_a...  244 us
    ppermute x4, waiting for transfers between devices, body(): arrived = lax.ppermute(block, 'res', moves)  63.8 us
    ppermute x2, waiting for transfers between devices, body(): right_other = [lax.ppermute(right_own[t], 'res', across) for t in spans]  28.8 us
    all_to_all x6, starting transfers between devices, in_half(): lax.all_to_all(values, 'res', split_axis=split_axis, concat_axis=concat_a...  27.9 us
    dot_general x2, matrix products, factor(): jnp.einsum('rkd,dc->crk', normed, project_weight, preferred_element_type=...  23.7 us
    all_to_all x6, local copies, waits for them, and re-layouts, in_half(): lax.all_to_all(values, 'res', split_axis=split_axis, concat_axis=concat_a...  20.1 us
    dot_general x2, matrix products, factor(): jnp.einsum('rkd,dc->crk', normed, gating_weight, preferred_element_type=j...  19.5 us
    ppermute x5, waiting for transfers between devices, total_over(): values = values + lax.ppermute(values, axis_name, moves)  14.1 us
  transfers between devices with their start and end apart: 18, of which 15 were waited for; matrix products, arithmetic and copies ran while one was open for 16% of the time, Pallas kernels for 0%

profile of v4, /device:TPU:0, one launch (start us, length us, event | category | flops | bytes accessed | tf_op | source)
XLA Modules:
  0.0 582.6 jit_solution(13826407477626717286)
XLA Ops:
  2.1 3.8 convert_reduce_fusion
  5.9 5.5 fusion.3
  11.6 9.5 %fusion.51 = f32[48,384,128]{2,1,0:T(8,128)S(1)} fusion(bf16[128,128]{1,0:T(8,128)(2,1)S(1)} %copy-done.9, bf16[1,48,384,128]{3,2,1,0:T(8,128)(2,1)} %param.13, f32[128]{0:T(128)S(1)} %copy-done.13, f32[48,384]{1,0:T(8,128)S(1)} %get-tuple-element.69, f32[48,384]{1,0:T(8,128)S(1)} %broadcast_multiply_fusion.1), kind=kOutput, calls=%fused_computation.83 | convolution fusion | flops 615776256 | bytes 14336512 | tf_op jit(solution)/shard_map/rkd,dc->crk/dot_general | solution.py:72
  21.1 10.6 %fusion.26 = bf16[128,48,384]{0,2,1:T(8,128)(2,1)} fusion(f32[48,384]{1,0:T(8,128)S(1)} %get-tuple-element.70, f32[48,384,128]{2,1,0:T(8,128)S(1)} %fusion.51, bf16[128,128]{1,0:T(8,128)(2,1)S(1)} %copy-done.18, bf16[1,48,384,128]{3,2,1,0:T(8,128)(2,1)S(1)} %bitcast.159, f32[128]{0:T(128)S(1)} %copy-done.13, f32[48,384]{1,0:T(8,128)S(1)} %get-tuple-element.69, ...), kind=kOutput, calls=%fused_computation.48 | convolution fusion | flops 629932032 | bytes 19128832 | tf_op jit(solution)/shard_map/rkd,dc->crk/dot_general | solution.py:68
  31.7 7.0 %copy.100 = bf16[128,48,384]{2,1,0:T(8,128)(2,1)} copy(bf16[128,48,384]{0,2,1:T(8,128)(2,1)} %fusion.26) | data formatting | bytes 9437184 | tf_op jit(solution)/shard_map/convert_element_type | solution.py:74
  38.7 5.4 all-to-all-start
  45.0 10.0 %fusion.54 = f32[48,384,128]{2,1,0:T(8,128)} fusion(bf16[128,128]{1,0:T(8,128)(2,1)S(1)} %copy-done.10, bf16[1,48,384,128]{3,2,1,0:T(8,128)(2,1)} %param.13, f32[128]{0:T(128)S(1)} %copy-done.13, f32[48,384]{1,0:T(8,128)S(1)} %get-tuple-element.69, f32[48,384]{1,0:T(8,128)S(1)} %broadcast_multiply_fusion.1), kind=kOutput, calls=%fused_computation.86 | convolution fusion | flops 615776256 | bytes 14336512 | tf_op jit(solution)/shard_map/rkd,dc->crk/dot_general | solution.py:72
  55.0 43.4 %all-to-all-done = bf16[128,48,384]{2,1,0:T(8,128)(2,1)} async-done(((bf16[128,48,384]{2,1,0:T(8,128)(2,1)}), bf16[128,48,384]{2,1,0:T(8,128)(2,1)}, u32[]{:S(2)}, u32[]{:S(2)}) %all-to-all-start) | async-done | bytes 4718624 | tf_op jit(solution)/shard_map/all_to_all | solution.py:77
  98.4 4.9 all-to-all-start.2
  103.3 13.2 %fusion.25 = bf16[128,48,384]{0,2,1:T(8,128)(2,1)} fusion(f32[48,384]{1,0:T(8,128)S(1)} %get-tuple-element.70, f32[48,384,128]{2,1,0:T(8,128)} %fusion.54, bf16[128,128]{1,0:T(8,128)(2,1)S(1)} %copy-done.19, bf16[1,48,384,128]{3,2,1,0:T(8,128)(2,1)} %param.13, f32[128]{0:T(128)S(1)} %copy-done.13, f32[48,384]{1,0:T(8,128)S(1)} %get-tuple-element.69, ...), kind=kOutput, calls=%fused_computation.47 | convolution fusion | flops 629932032 | bytes 19128832 | tf_op jit(solution)/shard_map/rkd,dc->crk/dot_general | solution.py:68
  116.5 5.4 copy.101
  121.9 7.0 %copy.102 = bf16[128,48,384]{2,1,0:T(8,128)(2,1)} copy(bf16[128,48,384]{0,2,1:T(8,128)(2,1)} %fusion.25) | data formatting | bytes 9437184 | tf_op jit(solution)/shard_map/optimization_barrier | solution.py:88
  128.8 5.3 all-to-all-start.1
  134.1 5.2 fusion.69
  139.3 2.9 collective-permute-start
  142.3 9.6 %add_divide_fusion = f32[48,384,128]{2,1,0:T(8,128)} fusion(bf16[128,128]{1,0:T(8,128)(2,1)S(1)} %copy-done.20, bf16[1,48,384,128]{3,2,1,0:T(8,128)(2,1)S(1)} %bitcast.161, f32[128]{0:T(128)S(1)} %copy-done.13, f32[48,384]{1,0:T(8,128)S(1)} %get-tuple-element.69, f32[48,384]{1,0:T(8,128)S(1)} %broadcast_multiply_fusion.1), kind=kOutput, calls=%fused_computation.12 | convolution fusion | flops 622854144 | bytes 14336512 | tf_op jit(solution)/shard_map/rkd,de->rke/dot_general | solution.py:94
  153.5 80.3 %all-to-all-done.1 = bf16[128,48,384]{2,1,0:T(8,128)(2,1)} async-done(((bf16[128,48,384]{2,1,0:T(8,128)(2,1)}), bf16[128,48,384]{2,1,0:T(8,128)(2,1)}, u32[]{:S(2)}, u32[]{:S(2)}) %all-to-all-start.1) | async-done | bytes 4718624 | tf_op jit(solution)/shard_map/all_to_all | solution.py:77
  233.8 3.3 copy.103
  237.2 4.3 fusion.68
  244.4 2.7 convolution_convert_fusion.2
  249.1 4.4 all-to-all-start.4
  253.4 3.4 copy.106
  256.9 15.2 %all-to-all-done.4 = bf16[16,192,192]{2,0,1:T(8,128)(2,1)} async-done(((bf16[16,192,192]{2,0,1:T(8,128)(2,1)}), bf16[16,192,192]{2,0,1:T(8,128)(2,1)}, u32[]{:S(2)}, u32[]{:S(2)}) %all-to-all-start.4) | async-done | bytes 1179680 | tf_op jit(solution)/shard_map/all_to_all | solution.py:77
  272.0 3.7 all-to-all-start.3
  277.8 3.5 copy.113
  281.3 3.1 copy.111
  284.4 61.8 %all-to-all-done.3 = bf16[32,192,192]{2,0,1:T(8,128)(2,1)S(1)} async-done(((bf16[32,192,192]{2,0,1:T(8,128)(2,1)}), bf16[32,192,192]{2,0,1:T(8,128)(2,1)S(1)}, u32[]{:S(2)}, u32[]{:S(2)}) %all-to-all-start.3) | async-done | bytes 2359328 | tf_op jit(solution)/shard_map/all_to_all | solution.py:77
  347.8 3.8 copy.107
  351.7 28.1 %collective-permute-done.1 = bf16[16,192,384]{2,1,0:T(8,128)(2,1)} collective-permute-done((bf16[16,192,384]{2,1,0:T(8,128)(2,1)}, bf16[16,192,384]{2,1,0:T(8,128)(2,1)}, u32[]{:S(2)}, u32[]{:S(2)}) %collective-permute-start.1) | collective-permute-done | bytes 2359328 | tf_op jit(solution)/shard_map/ppermute | solution.py:91
  379.8 2.7 convolution_convert_fusion.1
  384.5 4.7 all-to-all-start.5
  390.8 16.3 %all-to-all-done.5 = bf16[16,192,192]{2,0,1:T(8,128)(2,1)} async-done(((bf16[16,192,192]{2,0,1:T(8,128)(2,1)}), bf16[16,192,192]{2,0,1:T(8,128)(2,1)}, u32[]{:S(2)}, u32[]{:S(2)}) %all-to-all-start.5) | async-done | bytes 1179680 | tf_op jit(solution)/shard_map/all_to_all | solution.py:77
  413.2 3.9 fusion.14
  418.2 2.6 constant_dynamic-update-slice_fusion.2
  423.0 3.0 copy.118
  426.0 4.5 all-to-all-start.6
  430.6 6.4 %constant_dynamic-update-slice_fusion.1 = (bf16[48,384,128]{2,1,0:T(8,128)(2,1)}, bf16[48,192,128]{2,1,0:T(8,128)(2,1)S(1)}) fusion(bf16[48,384,128]{2,1,0:T(8,128)(2,1)} %copy-done.2, s32[]{:T(128)S(6)} %select_n.82, bf16[128,128]{1,0:T(8,128)(2,1)S(1)} %copy-done, bf16[128,48,192]{2,1,0:T(8,128)(2,1)S(1)} %copy-done.5, ...), kind=kOutput, calls=%fused_computation.96 | convolution fusion | flops 306708480 | bytes 14188548 | tf_op jit(solution)/shard_map/crk,cd->rkd/dot_general | solution.py:106
  440.3 2.4 collective-permute-start.3
  442.7 2.7 collective-permute-start.4
  447.6 27.6 %all-to-all-done.6 = bf16[48,192,128]{2,0,1:T(8,128)(2,1)} async-done(((bf16[48,192,128]{2,0,1:T(8,128)(2,1)}), bf16[48,192,128]{2,0,1:T(8,128)(2,1)}, u32[]{:S(2)}, u32[]{:S(2)}) %all-to-all-start.6) | async-done | bytes 2359328 | tf_op jit(solution)/shard_map/all_to_all | solution.py:77
  479.2 8.0 %collective-permute-done.3 = bf16[48,48,128]{2,1,0:T(8,128)(2,1)S(1)} collective-permute-done((bf16[48,48,128]{2,1,0:T(8,128)(2,1)}, bf16[48,48,128]{2,1,0:T(8,128)(2,1)S(1)}, u32[]{:S(2)}, u32[]{:S(2)}) %collective-permute-start.3) | collective-permute-done | bytes 589856 | tf_op jit(solution)/shard_map/ppermute | solution.py:141
  487.4 11.4 %collective-permute-done.4 = bf16[48,48,128]{2,1,0:T(8,128)(2,1)S(1)} collective-permute-done((bf16[48,48,128]{2,1,0:T(8,128)(2,1)}, bf16[48,48,128]{2,1,0:T(8,128)(2,1)S(1)}, u32[]{:S(2)}, u32[]{:S(2)}) %collective-permute-start.4) | collective-permute-done | bytes 589856 | tf_op jit(solution)/shard_map/ppermute | solution.py:141
  499.0 44.3 %collective-permute-done.5 = bf16[48,48,128]{2,1,0:T(8,128)(2,1)S(1)} collective-permute-done((bf16[48,48,128]{2,1,0:T(8,128)(2,1)S(1)}, bf16[48,48,128]{2,1,0:T(8,128)(2,1)S(1)}, u32[]{:S(2)}, u32[]{:S(2)}) %collective-permute-start.5) | collective-permute-done | bytes 589856 | tf_op jit(solution)/shard_map/ppermute | solution.py:141
  548.6 3.9 convert_reduce_fusion.2
  555.6 3.9 collective-permute-done.6
  559.6 4.2 collective-permute-done.7
  563.8 4.8 collective-permute-done.8
  571.4 5.3 convert_bitcast_fusion.1
  (141 shorter events, 49.7 us)
Async XLA Ops:
  0.6 417.5 %copy-start = (bf16[128,128]{1,0:T(8,128)(2,1)S(1)}, bf16[128,128]{1,0:T(8,128)(2,1)}, u32[]{:S(2)}) copy-start(bf16[128,128]{1,0:T(8,128)(2,1)} %param.23) | copy-start | bytes 98308
  2.0 9.5 %copy-start.11 = (f32[384]{0:T(512)}, f32[384]{0:T(512)S(1)}, u32[]{:S(2)}) copy-start(f32[384]{0:T(512)S(1)} %convert_reduce_fusion.3) | copy-start | bytes 4612
  2.0 3.9 copy-start.1
  2.1 9.5 %copy-start.9 = (bf16[128,128]{1,0:T(8,128)(2,1)S(1)}, bf16[128,128]{1,0:T(8,128)(2,1)}, u32[]{:S(2)}) copy-start(bf16[128,128]{1,0:T(8,128)(2,1)} %param.20) | copy-start | bytes 98308
  2.1 9.5 %copy-start.13 = (f32[128]{0:T(128)S(1)}, f32[128]{0:T(128)}, u32[]{:S(2)}) copy-start(f32[128]{0:T(128)} %param.16) | copy-start | bytes 1540
  5.9 15.2 %slice-start = ((s8[4718592]{0:T(1024)(128)(4,1)}), s8[524288]{0:T(1024)(128)(4,1)S(1)}, s32[]{:S(2)}) async-start(s8[4718592]{0:T(1024)(128)(4,1)} %bitcast.158), calls=%async_computation.7 | async-start | bytes 1048576
  11.5 9.6 %copy-start.15 = (f32[48]{0:T(128)}, f32[48]{0:T(128)S(1)}, u32[]{:S(2)}) copy-start(f32[48]{0:T(128)S(1)} %fusion.58) | copy-start | bytes 580
  11.6 9.5 %slice-start.1 = ((s8[4718592]{0:T(1024)(128)(4,1)}), s8[4194304]{0:T(1024)(128)(4,1)S(1)}, s32[]{:S(2)}) async-start(s8[4718592]{0:T(1024)(128)(4,1)} %bitcast.158), calls=%async_computation.8 | async-start | bytes 8388608
  11.6 9.5 %copy-start.18 = (bf16[128,128]{1,0:T(8,128)(2,1)S(1)}, bf16[128,128]{1,0:T(8,128)(2,1)}, u32[]{:S(2)}) copy-start(bf16[128,128]{1,0:T(8,128)(2,1)} %param.19) | copy-start | bytes 98308
  38.7 5.4 copy-start.7
  38.7 6.4 %copy-start.10 = (bf16[128,128]{1,0:T(8,128)(2,1)S(1)}, bf16[128,128]{1,0:T(8,128)(2,1)}, u32[]{:S(2)}) copy-start(bf16[128,128]{1,0:T(8,128)(2,1)} %param.18) | copy-start | bytes 98308
  38.7 59.7 %all-to-all-start = ((bf16[128,48,384]{2,1,0:T(8,128)(2,1)}), bf16[128,48,384]{2,1,0:T(8,128)(2,1)}, u32[]{:S(2)}, u32[]{:S(2)}) async-start(bf16[128,48,384]{2,1,0:T(8,128)(2,1)} %copy.100), calls=%async_computation | async-start | bytes 9437184 | tf_op jit(solution)/shard_map/all_to_all | solution.py:77
  45.0 58.3 %copy-start.19 = (bf16[128,128]{1,0:T(8,128)(2,1)S(1)}, bf16[128,128]{1,0:T(8,128)(2,1)}, u32[]{:S(2)}) copy-start(bf16[128,128]{1,0:T(8,128)(2,1)} %param.17) | copy-start | bytes 98308
  98.4 30.4 %all-to-all-start.2 = ((s32[8,1,2304]{2,1,0:T(1,128)}), s32[8,1,2304]{2,1,0:T(1,128)S(1)}, u32[]{:S(2)}, u32[]{:S(2)}) async-start(s32[8,1,2304]{2,1,0:T(1,128)} %reshape.137), calls=%async_computation.2 | async-start | bytes 147456 | tf_op jit(solution)/shard_map/all_to_all | solution.py:53
  128.8 13.4 %slice-start.2 = ((s8[4718592]{0:T(1024)(128)(4,1)}), s8[524288]{0:T(1024)(128)(4,1)S(1)}, s32[]{:S(2)}) async-start(s8[4718592]{0:T(1024)(128)(4,1)} %bitcast.160), calls=%async_computation.9 | async-start | bytes 1048576
  128.8 105.0 %all-to-all-start.1 = ((bf16[128,48,384]{2,1,0:T(8,128)(2,1)}), bf16[128,48,384]{2,1,0:T(8,128)(2,1)}, u32[]{:S(2)}, u32[]{:S(2)}) async-start(bf16[128,48,384]{2,1,0:T(8,128)(2,1)} %copy.102), calls=%async_computation.1 | async-start | bytes 9437184 | tf_op jit(solution)/shard_map/all_to_all | solution.py:77
  134.1 8.2 %slice-start.3 = ((s8[4718592]{0:T(1024)(128)(4,1)}), s8[4194304]{0:T(1024)(128)(4,1)S(1)}, s32[]{:S(2)}) async-start(s8[4718592]{0:T(1024)(128)(4,1)} %bitcast.160), calls=%async_computation.10 | async-start | bytes 8388608
  134.1 8.1 %copy-start.20 = (bf16[128,128]{1,0:T(8,128)(2,1)S(1)}, bf16[128,128]{1,0:T(8,128)(2,1)}, u32[]{:S(2)}) copy-start(bf16[128,128]{1,0:T(8,128)(2,1)} %param.21) | copy-start | bytes 98308
  139.3 104.7 %collective-permute-start = (bf16[16,192,384]{2,1,0:T(8,128)(2,1)}, bf16[16,192,384]{2,1,0:T(8,128)(2,1)}, u32[]{:S(2)}, u32[]{:S(2)}) collective-permute-start(bf16[16,192,384]{2,1,0:T(8,128)(2,1)} %get-tuple-element.54), channel_id=1, source_target_pairs={{0,16},{4,20},{8,24},{12,28},{16,0},{20,4},{24,8},{28,12},{1,17},{... | collective-permute-start | bytes 7077896 | tf_op jit(solution)/shard_map/ppermute | solution.py:91
  233.8 7.7 %slice-start.6 = ((s8[4718592]{0:T(1024)(128)(4,1)}), s8[4194304]{0:T(1024)(128)(4,1)S(1)}, s32[]{:S(2)}) async-start(s8[4718592]{0:T(1024)(128)(4,1)} %bitcast.168), calls=%async_computation.13 | async-start | bytes 8388608
  237.1 4.3 slice-start.7
  249.1 23.0 %all-to-all-start.4 = ((bf16[16,192,192]{2,0,1:T(8,128)(2,1)}), bf16[16,192,192]{2,0,1:T(8,128)(2,1)}, u32[]{:S(2)}, u32[]{:S(2)}) async-start(bf16[16,192,192]{2,0,1:T(8,128)(2,1)} %copy.109), calls=%async_computation.4 | async-start | bytes 3145728 | tf_op jit(solution)/shard_map/all_to_all | solution.py:77
  272.0 74.1 %all-to-all-start.3 = ((bf16[32,192,192]{2,0,1:T(8,128)(2,1)}), bf16[32,192,192]{2,0,1:T(8,128)(2,1)S(1)}, u32[]{:S(2)}, u32[]{:S(2)}) async-start(bf16[32,192,192]{2,0,1:T(8,128)(2,1)} %copy.106), calls=%async_computation.3 | async-start | bytes 6291456 | tf_op jit(solution)/shard_map/all_to_all | solution.py:77
  275.7 104.0 %collective-permute-start.1 = (bf16[16,192,384]{2,1,0:T(8,128)(2,1)}, bf16[16,192,384]{2,1,0:T(8,128)(2,1)}, u32[]{:S(2)}, u32[]{:S(2)}) collective-permute-start(bf16[16,192,384]{2,1,0:T(8,128)(2,1)} %get-tuple-element.53), channel_id=1, source_target_pairs={{0,16},{4,20},{8,24},{12,28},{16,0},{20,4},{24,8},{28,12},{1,17},{... | collective-permute-start | bytes 7077896 | tf_op jit(solution)/shard_map/ppermute | solution.py:91
  347.8 31.9 %copy-start.6 = (bf16[16,4,48,384]{3,2,1,0:T(8,128)(2,1)S(1)}, bf16[16,4,48,384]{3,2,1,0:T(8,128)(2,1)}, u32[]{:S(2)}) copy-start(bf16[16,4,48,384]{3,2,1,0:T(8,128)(2,1)} %copy.113) | copy-start | bytes 7077892
  384.5 22.6 %all-to-all-start.5 = ((bf16[16,192,192]{2,0,1:T(8,128)(2,1)}), bf16[16,192,192]{2,0,1:T(8,128)(2,1)}, u32[]{:S(2)}, u32[]{:S(2)}) async-start(bf16[16,192,192]{2,0,1:T(8,128)(2,1)} %copy.114), calls=%async_computation.5 | async-start | bytes 3145728 | tf_op jit(solution)/shard_map/all_to_all | solution.py:77
  407.1 4.2 copy-start.3
  411.3 6.9 %slice-start.4 = ((s8[4718592]{0:T(1024)(128)(4,1)}), s8[4194304]{0:T(1024)(128)(4,1)S(1)}, s32[]{:S(2)}) async-start(s8[4718592]{0:T(1024)(128)(4,1)} %bitcast.162), calls=%async_computation.11 | async-start | bytes 8388608
  412.1 6.1 %slice-start.10 = ((s8[9437184]{0:T(1024)(128)(4,1)}), s8[4194304]{0:T(1024)(128)(4,1)S(1)}, s32[]{:S(2)}) async-start(s8[9437184]{0:T(1024)(128)(4,1)} %bitcast.182), calls=%async_computation.17 | async-start | bytes 8388608
  413.1 5.0 slice-start.5
  413.2 5.0 slice-start.11
  413.2 5.0 slice-start.12
  423.0 7.6 %copy-start.5 = (bf16[128,48,192]{2,1,0:T(8,128)(2,1)S(1)}, bf16[128,48,192]{2,1,0:T(8,128)(2,1)}, u32[]{:S(2)}) copy-start(bf16[128,48,192]{2,1,0:T(8,128)(2,1)} %get-tuple-element.61) | copy-start | bytes 7077892
  426.0 49.2 %all-to-all-start.6 = ((bf16[48,192,128]{2,0,1:T(8,128)(2,1)}), bf16[48,192,128]{2,0,1:T(8,128)(2,1)}, u32[]{:S(2)}, u32[]{:S(2)}) async-start(bf16[48,192,128]{2,0,1:T(8,128)(2,1)} %copy.118), calls=%async_computation.6 | async-start | bytes 4718592 | tf_op jit(solution)/shard_map/all_to_all | solution.py:77
  438.5 40.5 %collective-permute-start.2 = (bf16[48,48,128]{2,1,0:T(8,128)(2,1)}, bf16[48,48,128]{2,1,0:T(8,128)(2,1)S(1)}, u32[]{:S(2)}, u32[]{:S(2)}) collective-permute-start(bf16[48,48,128]{2,1,0:T(8,128)(2,1)} %get-tuple-element.58), channel_id=1, source_target_pairs={{0,16},{4,20},{8,24},{12,28},{16,0},{20,4},{24,8},{28,12},{1,17},{... | collective-permute-start | bytes 1769480 | tf_op jit(solution)/shard_map/ppermute | solution.py:141
  440.3 46.9 %collective-permute-start.3 = (bf16[48,48,128]{2,1,0:T(8,128)(2,1)}, bf16[48,48,128]{2,1,0:T(8,128)(2,1)S(1)}, u32[]{:S(2)}, u32[]{:S(2)}) collective-permute-start(bf16[48,48,128]{2,1,0:T(8,128)(2,1)} %get-tuple-element.57), channel_id=1, source_target_pairs={{0,20},{4,24},{8,28},{12,16},{16,4},{20,8},{24,12},{28,0},{1,21},{... | collective-permute-start | bytes 1769480 | tf_op jit(solution)/shard_map/ppermute | solution.py:141
  442.7 56.1 %collective-permute-start.4 = (bf16[48,48,128]{2,1,0:T(8,128)(2,1)}, bf16[48,48,128]{2,1,0:T(8,128)(2,1)S(1)}, u32[]{:S(2)}, u32[]{:S(2)}) collective-permute-start(bf16[48,48,128]{2,1,0:T(8,128)(2,1)} %get-tuple-element.56), channel_id=1, source_target_pairs={{0,24},{4,28},{8,16},{12,20},{16,8},{20,12},{24,0},{28,4},{1,25},{... | collective-permute-start | bytes 1769480 | tf_op jit(solution)/shard_map/ppermute | solution.py:141
  445.4 97.9 %collective-permute-start.5 = (bf16[48,48,128]{2,1,0:T(8,128)(2,1)S(1)}, bf16[48,48,128]{2,1,0:T(8,128)(2,1)S(1)}, u32[]{:S(2)}, u32[]{:S(2)}) collective-permute-start(bf16[48,48,128]{2,1,0:T(8,128)(2,1)S(1)} %get-tuple-element.55), channel_id=1, source_target_pairs={{0,28},{4,16},{8,20},{12,24},{16,12},{20,0},{24,4},{28,8},{1,29},{... | collective-permute-start | bytes 1769480 | tf_op jit(solution)/shard_map/ppermute | solution.py:141
  477.5 66.0 %slice-start.8 = ((s8[4718592]{0:T(1024)(128)(4,1)}), s8[4194304]{0:T(1024)(128)(4,1)S(1)}, s32[]{:S(2)}) async-start(s8[4718592]{0:T(1024)(128)(4,1)} %bitcast.172), calls=%async_computation.15 | async-start | bytes 8388608
  478.6 64.9 %slice-start.9 = ((s8[4718592]{0:T(1024)(128)(4,1)}), s8[524288]{0:T(1024)(128)(4,1)S(1)}, s32[]{:S(2)}) async-start(s8[4718592]{0:T(1024)(128)(4,1)} %bitcast.172), calls=%async_computation.16 | async-start | bytes 1048576
  478.6 64.9 %copy-start.8 = (bf16[128,64]{0,1:T(8,128)(2,1)S(1)}, bf16[128,64]{0,1:T(8,128)(2,1)}, u32[]{:S(2)}) copy-start(bf16[128,64]{0,1:T(8,128)(2,1)} %param.24) | copy-start | bytes 49156
  478.7 64.9 %copy-start.14 = (f32[64]{0:T(128)S(1)}, f32[64]{0:T(128)}, u32[]{:S(2)}) copy-start(f32[64]{0:T(128)} %param.25) | copy-start | bytes 772
  545.6 2.3 copy-start.12
  555.5 4.0 collective-permute-start.6
  559.5 4.3 collective-permute-start.7
  563.8 4.9 collective-permute-start.8
  568.7 1.2 collective-permute-start.9
  569.9 6.9 %collective-permute-start.10 = (f32[66,128]{1,0:T(8,128)S(1)}, f32[66,128]{1,0:T(8,128)S(1)}, u32[]{:S(2)}, u32[]{:S(2)}) collective-permute-start(f32[66,128]{1,0:T(8,128)S(1)} %add.218), channel_id=1, source_target_pairs={{0,2},{1,3},{2,0},{3,1},{4,6},{5,7},{6,4},{7,5},{8,10},{9,11},{10,... | collective-permute-start | bytes 101384 | tf_op jit(solution)/shard_map/ppermute | solution.py:23
  (4 other events, 8.0 us)

commit v5 on v1

--- a/solution.py
+++ b/solution.py
@@ -9,6 +9,18 @@
     centered = values - average
     variance = jnp.mean(centered * centered, axis=reduce_axis, keepdims=True)
     return centered * lax.rsqrt(variance + 1e-05)
+
+
+def total_over(values, axis_name):
+    size = lax.axis_size(axis_name)
+    if size & (size - 1):
+        return lax.psum(values, axis_name)
+    step = 1
+    while step < size:
+        moves = [(d, d ^ step) for d in range(size)]
+        values = values + lax.ppermute(values, axis_name, moves)
+        step *= 2
+    return values
 
 
 def body(
@@ -92,9 +104,19 @@
     bias_part = jnp.sum(dlogits.astype(jnp.float32), axis=(1, 2))
     loss_part = jnp.sum(pair_mask * (log_total[0] - jnp.sum(target_hot * logits, axis=0)))
     count_part = jnp.sum(pair_mask)
-    head_total, bias_total, loss_total, count = lax.psum(
-        (head_part, bias_part, loss_part, count_part), ("res", "rep")
+    head_shape = head_part.shape
+    packed = jnp.concatenate(
+        [
+            head_part.reshape(-1, 128),
+            jnp.pad(bias_part, (0, 128 - bias_part.shape[0]))[None],
+            jnp.pad(jnp.stack([loss_part, count_part]), (0, 126))[None],
+        ],
+        axis=0,
     )
+    packed = total_over(total_over(packed, "res"), "rep")
+    head_total = packed[:-2].reshape(head_shape)
+    bias_total = packed[-2, : bias_part.shape[0]]
+    loss_total, count = packed[-1, 0], packed[-1, 1]
     mean_loss = jnp.reshape(loss_total / count, (1,))
     return (updated[None], pair_grad[None], head_total / count, bias_total / count, mean_loss)
 

time: 601 us -> 580 us (0.965)
  blocking collectives: 38.4 us -> 0 us
  waiting for transfers between devices: 381 us -> 393 us
    psum x1 -> x0, blocking collectives: 38.4 us -> none  [body(): lax.psum((head_part, bias_part, loss_part, count_part), ('res', 'rep'))]
    ppermute x0 -> x5, waiting for transfers between devices: none -> 11.6 us  [total_over(): values = values + lax.ppermute(values, axis_name, moves)]
  transfers between devices with their start and end apart: 5 -> 10, of which waited for: 4 -> 8; matrix products, arithmetic and copies ran while one was open for 11% -> 12% of each run, Pallas kernels for 0% -> 0%
where the time goes in v5:
time: 580 us; the launch traced here: 579 us
  waiting for transfers between devices  393 us (68%)
  matrix products  62.8 us (11%)
  local copies, waits for them, and re-layouts  54.3 us (9%)
  other arithmetic  35 us (6%)
  starting transfers between devices  30.3 us (5%)
    all_to_all x1, waiting for transfers between devices, body(): lax.all_to_all(by_units, 'res', split_axis=1, concat_axis=0, tiled=True)  103 us
    all_to_all x1, waiting for transfers between devices, body(): lax.all_to_all(updated, 'res', split_axis=1, concat_axis=0, tiled=True)  103 us
    all_to_all x1, waiting for transfers between devices, body(): lax.all_to_all(left_factor, 'res', split_axis=0, concat_axis=1, tiled=True)  98.5 us
    all_to_all x1, waiting for transfers between devices, body(): lax.all_to_all(right_factor, 'res', split_axis=0, concat_axis=1, tiled=True)  77.5 us
    dot_general x2, matrix products, factor(): jnp.einsum('rkd,dc->crk', normed, project_weight, preferred_element_type=...  21.1 us
    dot_general x2, matrix products, factor(): jnp.einsum('rkd,dc->crk', normed, gating_weight, preferred_element_type=j...  18.9 us
    convert_element_type x2, local copies, waits for them, and re-layouts, factor(): return (gated * projected * pair_mask[None]).astype(jnp.bfloat16)  14.1 us
    ppermute x5, waiting for transfers between devices, total_over(): values = values + lax.ppermute(values, axis_name, moves)  11.6 us
  transfers between devices with their start and end apart: 10, of which 8 were waited for; matrix products, arithmetic and copies ran while one was open for 12% of the time, Pallas kernels for 0%

profile of v5, /device:TPU:0, one launch (start us, length us, event | category | flops | bytes accessed | tf_op | source)
XLA Modules:
  0.0 578.9 jit_solution(18369580697729004707)
XLA Ops:
  2.1 3.8 convert_reduce_fusion
  5.9 5.5 fusion.4
  11.6 9.5 %fusion.31 = f32[48,384,128]{2,1,0:T(8,128)S(1)} fusion(bf16[128,128]{1,0:T(8,128)(2,1)S(1)} %copy-done, bf16[1,48,384,128]{3,2,1,0:T(8,128)(2,1)} %param.13, f32[128]{0:T(128)S(1)} %copy-done.11, f32[48,384]{1,0:T(8,128)S(1)} %get-tuple-element.32, f32[48,384]{1,0:T(8,128)S(1)} %broadcast_multiply_fusion.2), kind=kOutput, calls=%fused_computation.60 | convolution fusion | flops 615776256 | bytes 14336512 | tf_op jit(solution)/shard_map/rkd,dc->crk/dot_general | solution.py:59
  21.1 10.6 %fusion.24 = bf16[128,48,384]{0,2,1:T(8,128)(2,1)} fusion(f32[48,384]{1,0:T(8,128)S(1)} %get-tuple-element.33, f32[48,384,128]{2,1,0:T(8,128)S(1)} %fusion.31, bf16[128,128]{1,0:T(8,128)(2,1)S(1)} %copy-done.16, bf16[1,48,384,128]{3,2,1,0:T(8,128)(2,1)S(1)} %bitcast.138, f32[128]{0:T(128)S(1)} %copy-done.11, f32[48,384]{1,0:T(8,128)S(1)} %get-tuple-element.32, ...), kind=kOutput, calls=%fused_computation.42 | convolution fusion | flops 629932032 | bytes 19128832 | tf_op jit(solution)/shard_map/rkd,dc->crk/dot_general | solution.py:55
  31.7 7.1 %copy.55 = bf16[128,48,384]{2,1,0:T(8,128)(2,1)} copy(bf16[128,48,384]{0,2,1:T(8,128)(2,1)} %fusion.24) | data formatting | bytes 9437184 | tf_op jit(solution)/shard_map/convert_element_type | solution.py:61
  38.8 7.4 %all-to-all-start.1 = ((bf16[128,48,384]{2,1,0:T(8,128)(2,1)}), bf16[128,48,384]{2,1,0:T(8,128)(2,1)}, u32[]{:S(2)}, u32[]{:S(2)}) async-start(bf16[128,48,384]{2,1,0:T(8,128)(2,1)} %copy.55), calls=%async_computation.1 | async-start | bytes 9437184 | tf_op jit(solution)/shard_map/all_to_all | solution.py:67
  46.2 9.5 %fusion.34 = f32[48,384,128]{2,1,0:T(8,128)S(1)} fusion(bf16[128,128]{1,0:T(8,128)(2,1)S(1)} %copy-done.7, bf16[1,48,384,128]{3,2,1,0:T(8,128)(2,1)} %param.13, f32[128]{0:T(128)S(1)} %copy-done.11, f32[48,384]{1,0:T(8,128)S(1)} %get-tuple-element.32, f32[48,384]{1,0:T(8,128)S(1)} %broadcast_multiply_fusion.2), kind=kOutput, calls=%fused_computation.63 | convolution fusion | flops 615776256 | bytes 14336512 | tf_op jit(solution)/shard_map/rkd,dc->crk/dot_general | solution.py:59
  55.7 10.6 %fusion.23 = bf16[128,48,384]{0,2,1:T(8,128)(2,1)} fusion(f32[48,384]{1,0:T(8,128)S(1)} %get-tuple-element.33, f32[48,384,128]{2,1,0:T(8,128)S(1)} %fusion.34, bf16[128,128]{1,0:T(8,128)(2,1)S(1)} %copy-done.17, bf16[1,48,384,128]{3,2,1,0:T(8,128)(2,1)S(1)} %bitcast.140, f32[128]{0:T(128)S(1)} %copy-done.11, f32[48,384]{1,0:T(8,128)S(1)} %get-tuple-element.32, ...), kind=kOutput, calls=%fused_computation.41 | convolution fusion | flops 629932032 | bytes 19128832 | tf_op jit(solution)/shard_map/rkd,dc->crk/dot_general | solution.py:55
  66.3 7.0 %copy.53 = bf16[128,48,384]{2,1,0:T(8,128)(2,1)} copy(bf16[128,48,384]{0,2,1:T(8,128)(2,1)} %fusion.23) | data formatting | bytes 9437184 | tf_op jit(solution)/shard_map/convert_element_type | solution.py:61
  73.3 77.5 %all-to-all-done.1 = bf16[128,48,384]{2,1,0:T(8,128)(2,1)} async-done(((bf16[128,48,384]{2,1,0:T(8,128)(2,1)}), bf16[128,48,384]{2,1,0:T(8,128)(2,1)}, u32[]{:S(2)}, u32[]{:S(2)}) %all-to-all-start.1) | async-done | bytes 4718624 | tf_op jit(solution)/shard_map/all_to_all | solution.py:67
  150.7 4.6 all-to-all-start
  155.4 5.2 copy.56
  160.6 98.5 %all-to-all-done = bf16[128,48,384]{2,1,0:T(8,128)(2,1)} async-done(((bf16[128,48,384]{2,1,0:T(8,128)(2,1)}), bf16[128,48,384]{2,1,0:T(8,128)(2,1)}, u32[]{:S(2)}, u32[]{:S(2)}) %all-to-all-start) | async-done | bytes 4718624 | tf_op jit(solution)/shard_map/all_to_all | solution.py:66
  259.1 3.2 copy.54
  262.8 3.4 convolution_convert_fusion
  266.2 5.0 copy.57
  271.2 4.7 all-to-all-start.2
  276.2 0.8 reshape.120
  277.0 102.7 %all-to-all-done.2 = bf16[16,384,384]{2,0,1:T(8,128)(2,1)} async-done(((bf16[16,384,384]{2,0,1:T(8,128)(2,1)}), bf16[16,384,384]{2,0,1:T(8,128)(2,1)}, u32[]{:S(2)}, u32[]{:S(2)}) %all-to-all-start.2) | async-done | bytes 4718624 | tf_op jit(solution)/shard_map/all_to_all | solution.py:72
  379.7 3.6 all-to-all-start.4
  383.3 3.5 copy.58
  387.5 1.0 convert_bitcast_fusion.1
  388.6 1.3 multiply_reduce_fusion
  389.9 4.5 copy.59
  394.5 5.0 fusion.11
  399.5 1.5 fusion.21
  401.0 9.3 %fusion.7 = bf16[48,384,128]{2,1,0:T(8,128)(2,1)S(1)} fusion(bf16[1,48,384,128]{3,2,1,0:T(8,128)(2,1)S(1)} %bitcast.142, f32[48,384,128]{2,1,0:T(8,128)S(1)} %fusion.21, bf16[128,128]{1,0:T(8,128)(2,1)S(1)} %copy-done.18, f32[128]{0:T(128)S(1)} %copy-done.11, f32[48,384]{1,0:T(8,128)S(1)} %get-tuple-element.32, f32[48,384]{1,0:T(8,128)S(1)} %broadcast_multiply_fusion.2), kind=kOutput, calls=%fused_computation.9 | convolution fusion | flops 632291328 | bytes 19055104 | tf_op jit(solution)/shard_map/rkd,de->rke/dot_general | solution.py:78
  410.3 2.2 copy-done.4
  412.5 5.2 copy.61
  417.7 6.0 %all-to-all-start.3 = ((bf16[48,384,128]{2,0,1:T(8,128)(2,1)}), bf16[48,384,128]{2,0,1:T(8,128)(2,1)}, u32[]{:S(2)}, u32[]{:S(2)}) async-start(bf16[48,384,128]{2,0,1:T(8,128)(2,1)} %copy.61), calls=%async_computation.3 | async-start | bytes 9437184 | tf_op jit(solution)/shard_map/all_to_all | solution.py:82
  424.2 0.8 reduce.5
  425.3 102.6 %all-to-all-done.3 = bf16[48,384,128]{2,0,1:T(8,128)(2,1)} async-done(((bf16[48,384,128]{2,0,1:T(8,128)(2,1)}), bf16[48,384,128]{2,0,1:T(8,128)(2,1)}, u32[]{:S(2)}, u32[]{:S(2)}) %all-to-all-start.3) | async-done | bytes 4718624 | tf_op jit(solution)/shard_map/all_to_all | solution.py:82
  527.9 7.4 %copy.62 = f32[48,8,48,128]{3,0,1,2:T(8,128)} copy(bf16[48,8,48,128]{3,0,2,1:T(8,128)(2,1)} %bitcast.44) | data formatting | bytes 14155776 | tf_op jit(solution)/shard_map/convert_element_type | solution.py:84
  535.2 5.4 fusion.8
  540.7 1.8 bitcast_reduce_fusion
  542.5 2.2 fusion.20
  545.4 3.8 convert_reduce_fusion.1
  549.3 1.5 convolution_bitcast_fusion
  550.8 1.4 fusion.41
  552.2 1.5 collective-permute-start
  553.7 2.5 collective-permute-done
  556.3 4.0 collective-permute-done.1
  560.3 0.8 collective-permute-start.2
  561.1 4.0 collective-permute-done.2
  565.3 1.1 collective-permute-done.3
  566.3 1.5 collective-permute-start.4
  567.9 5.3 convert_bitcast_fusion.2
  573.8 1.2 fusion.40
  (88 shorter events, 6.9 us)
Async XLA Ops:
  0.6 10.9 %copy-start = (bf16[128,128]{1,0:T(8,128)(2,1)S(1)}, bf16[128,128]{1,0:T(8,128)(2,1)}, u32[]{:S(2)}) copy-start(bf16[128,128]{1,0:T(8,128)(2,1)} %param.20) | copy-start | bytes 98308
  2.0 9.4 %copy-start.9 = (f32[384]{0:T(512)}, f32[384]{0:T(512)S(1)}, u32[]{:S(2)}) copy-start(f32[384]{0:T(512)S(1)} %convert_reduce_fusion.2) | copy-start | bytes 4612
  2.0 3.8 copy-start.2
  2.1 9.5 %copy-start.11 = (f32[128]{0:T(128)S(1)}, f32[128]{0:T(128)}, u32[]{:S(2)}) copy-start(f32[128]{0:T(128)} %param.16) | copy-start | bytes 1540
  5.9 15.2 %slice-start = ((s8[4718592]{0:T(1024)(128)(4,1)}), s8[524288]{0:T(1024)(128)(4,1)S(1)}, s32[]{:S(2)}) async-start(s8[4718592]{0:T(1024)(128)(4,1)} %bitcast.137), calls=%async_computation.5 | async-start | bytes 1048576
  11.5 9.6 %copy-start.13 = (f32[48]{0:T(128)}, f32[48]{0:T(128)S(1)}, u32[]{:S(2)}) copy-start(f32[48]{0:T(128)S(1)} %dynamic-slice_bitcast_fusion) | copy-start | bytes 580
  11.6 9.5 %slice-start.1 = ((s8[4718592]{0:T(1024)(128)(4,1)}), s8[4194304]{0:T(1024)(128)(4,1)S(1)}, s32[]{:S(2)}) async-start(s8[4718592]{0:T(1024)(128)(4,1)} %bitcast.137), calls=%async_computation.6 | async-start | bytes 8388608
  11.6 9.5 %copy-start.16 = (bf16[128,128]{1,0:T(8,128)(2,1)S(1)}, bf16[128,128]{1,0:T(8,128)(2,1)}, u32[]{:S(2)}) copy-start(bf16[128,128]{1,0:T(8,128)(2,1)} %param.19) | copy-start | bytes 98308
  38.8 7.4 %copy-start.7 = (bf16[128,128]{1,0:T(8,128)(2,1)S(1)}, bf16[128,128]{1,0:T(8,128)(2,1)}, u32[]{:S(2)}) copy-start(bf16[128,128]{1,0:T(8,128)(2,1)} %param.18) | copy-start | bytes 98308
  38.8 16.9 %slice-start.2 = ((s8[4718592]{0:T(1024)(128)(4,1)}), s8[524288]{0:T(1024)(128)(4,1)S(1)}, s32[]{:S(2)}) async-start(s8[4718592]{0:T(1024)(128)(4,1)} %bitcast.139), calls=%async_computation.7 | async-start | bytes 1048576
  38.8 111.9 %all-to-all-start.1 = ((bf16[128,48,384]{2,1,0:T(8,128)(2,1)}), bf16[128,48,384]{2,1,0:T(8,128)(2,1)}, u32[]{:S(2)}, u32[]{:S(2)}) async-start(bf16[128,48,384]{2,1,0:T(8,128)(2,1)} %copy.55), calls=%async_computation.1 | async-start | bytes 9437184 | tf_op jit(solution)/shard_map/all_to_all | solution.py:67
  46.2 9.5 %slice-start.3 = ((s8[4718592]{0:T(1024)(128)(4,1)}), s8[4194304]{0:T(1024)(128)(4,1)S(1)}, s32[]{:S(2)}) async-start(s8[4718592]{0:T(1024)(128)(4,1)} %bitcast.139), calls=%async_computation.8 | async-start | bytes 8388608
  46.2 9.5 %copy-start.17 = (bf16[128,128]{1,0:T(8,128)(2,1)S(1)}, bf16[128,128]{1,0:T(8,128)(2,1)}, u32[]{:S(2)}) copy-start(bf16[128,128]{1,0:T(8,128)(2,1)} %param.17) | copy-start | bytes 98308
  150.7 108.4 %all-to-all-start = ((bf16[128,48,384]{2,1,0:T(8,128)(2,1)}), bf16[128,48,384]{2,1,0:T(8,128)(2,1)}, u32[]{:S(2)}, u32[]{:S(2)}) async-start(bf16[128,48,384]{2,1,0:T(8,128)(2,1)} %copy.53), calls=%async_computation | async-start | bytes 9437184 | tf_op jit(solution)/shard_map/all_to_all | solution.py:66
  259.1 3.8 copy-start.3
  271.2 4.8 copy-start.5
  271.2 108.5 %all-to-all-start.2 = ((bf16[16,384,384]{2,0,1:T(8,128)(2,1)}), bf16[16,384,384]{2,0,1:T(8,128)(2,1)}, u32[]{:S(2)}, u32[]{:S(2)}) async-start(bf16[16,384,384]{2,0,1:T(8,128)(2,1)} %copy.57), calls=%async_computation.2 | async-start | bytes 9437184 | tf_op jit(solution)/shard_map/all_to_all | solution.py:72
  379.7 38.0 %all-to-all-start.4 = ((s32[8,1,2304]{2,1,0:T(1,128)}), s32[8,1,2304]{2,1,0:T(1,128)S(1)}, u32[]{:S(2)}, u32[]{:S(2)}) async-start(s32[8,1,2304]{2,1,0:T(1,128)} %reshape.120), calls=%async_computation.4 | async-start | bytes 147456 | tf_op jit(solution)/shard_map/all_to_all | solution.py:51
  389.9 4.6 copy-start.15
  389.9 11.1 %slice-start.4 = ((s8[4718592]{0:T(1024)(128)(4,1)}), s8[4194304]{0:T(1024)(128)(4,1)S(1)}, s32[]{:S(2)}) async-start(s8[4718592]{0:T(1024)(128)(4,1)} %bitcast.141), calls=%async_computation.9 | async-start | bytes 8388608
  394.5 5.0 copy-start.8
  394.5 6.5 %slice-start.5 = ((s8[4718592]{0:T(1024)(128)(4,1)}), s8[524288]{0:T(1024)(128)(4,1)S(1)}, s32[]{:S(2)}) async-start(s8[4718592]{0:T(1024)(128)(4,1)} %bitcast.141), calls=%async_computation.10 | async-start | bytes 1048576
  399.5 1.5 copy-start.18
  410.3 2.2 copy-start.4
  417.7 110.1 %all-to-all-start.3 = ((bf16[48,384,128]{2,0,1:T(8,128)(2,1)}), bf16[48,384,128]{2,0,1:T(8,128)(2,1)}, u32[]{:S(2)}, u32[]{:S(2)}) async-start(bf16[48,384,128]{2,0,1:T(8,128)(2,1)} %copy.61), calls=%async_computation.3 | async-start | bytes 9437184 | tf_op jit(solution)/shard_map/all_to_all | solution.py:82
  425.2 110.0 %slice-start.6 = ((s8[4718592]{0:T(1024)(128)(4,1)}), s8[524288]{0:T(1024)(128)(4,1)S(1)}, s32[]{:S(2)}) async-start(s8[4718592]{0:T(1024)(128)(4,1)} %bitcast.149), calls=%async_computation.11 | async-start | bytes 1048576
  527.9 7.4 %slice-start.7 = ((s8[4718592]{0:T(1024)(128)(4,1)}), s8[4194304]{0:T(1024)(128)(4,1)S(1)}, s32[]{:S(2)}) async-start(s8[4718592]{0:T(1024)(128)(4,1)} %bitcast.149), calls=%async_computation.12 | async-start | bytes 8388608
  535.2 5.4 copy-start.6
  535.2 5.4 copy-start.12
  542.5 2.2 copy-start.10
  542.5 2.2 copy-start.14
  552.2 4.0 collective-permute-start
  556.2 4.0 collective-permute-start.1
  560.3 4.9 collective-permute-start.2
  565.1 1.2 collective-permute-start.3
  566.3 6.9 %collective-permute-start.4 = (f32[66,128]{1,0:T(8,128)S(1)}, f32[66,128]{1,0:T(8,128)S(1)}, u32[]{:S(2)}, u32[]{:S(2)}) collective-permute-start(f32[66,128]{1,0:T(8,128)S(1)} %add.95), channel_id=1, source_target_pairs={{0,2},{1,3},{2,0},{3,1},{4,6},{5,7},{6,4},{7,5},{8,10},{9,11},{10,... | collective-permute-start | bytes 101384 | tf_op jit(solution)/shard_map/ppermute | solution.py:21
  567.9 9.9 %copy-start.1 = (bf16[128,128]{1,0:T(8,128)(2,1)S(1)}, bf16[128,128]{1,0:T(8,128)(2,1)}, u32[]{:S(2)}) copy-start(bf16[128,128]{1,0:T(8,128)(2,1)} %param.20) | copy-start | bytes 98308
